TPU v7x, 32 devices: a whole 2x2x4 slice. The times are simulated.
32 devices in a mesh: replica: 4 (over y, x), expert: 8 (over z, core).
Axes of the slice: x: 2, y: 2, z: 4, core: 2. Of those that a mesh axis runs over, the one named last changes fastest.
Arguments:
- moe_input: bfloat16 [512, 2048], P(('replica', 'expert')), may hold values from -6 to 6
- expert_ids: int32 [512, 8], P(('replica', 'expert')), may hold values from 0 to 7, all different within a row; in each aligned block of 16 rows (0 to 15, 16 to 31, ...) at most 16 rows name the same one
- route_weight: float32 [512, 8], P(('replica', 'expert')), may hold values from 0.05 to 0.5
- expert_slot: int32 [8], replicated, may hold values from 0 to 7, each once
- w_gate_up: bfloat16 [2048, 12288], P(None, ('replica', 'expert')), may hold values from -0.125 to 0.125
- w_down: bfloat16 [6144, 2048], P(('replica', 'expert')), may hold values from -0.21875 to 0.21875
- queries: bfloat16 [64, 8192], P(('replica', 'expert')), may hold values from -80 to 80
- incoming_key_value: bfloat16 [64, 1024], P(('replica', 'expert')), may hold values from -4 to 4
- key_value_pool: bfloat16 [512, 64, 1024], P(('replica', 'expert')), may hold values from -4 to 4
- block_owner: int32 [512], P(('replica', 'expert')), may hold values from 0 to 7, as said below
- block_tokens: int32 [512], P(('replica', 'expert')), may hold values from 1 to 64
Outputs:
- moe_out: bfloat16 [512, 2048], P(('replica', 'expert'))
- attn_out: bfloat16 [64, 8192], P(('replica', 'expert'))
Inputs may be any that keep to these rules, and one draw needn't show every extreme that they name: `expert_ids`: in the rows of one device no expert is named by more than 16 rows, a bound that some block reaches. `expert_slot`: each slot hosts one expert. `block_owner`: on every device at most 2 blocks are owned by requests of any one other replica, and exactly 2 for some other replica.
All inputs are finite; a program needn't handle non-finite values.
Results may differ from a plain program's by a relative error of at most 0.0058.
Values may be sent and summed in bfloat16 or wider, within the bound.
A program may use at most 64 MiB of HBM per device.

v0:
```python
import math

import jax
import jax.numpy as jnp
from jax import lax
from jax.sharding import PartitionSpec as P

QUART = 4
QUERY_HEADS = 64
KEY_VALUE_HEADS = 4
HEAD_DIMENSION = 128
DEVICE_REQUESTS = 2
DEVICE_BLOCKS = 16
BLOCK_SLOTS = 64
MIG = 2


HIGHEST = lax.Precision.HIGHEST


def partial_state(query_rows, rows, mask, scale):
    heads_kv = query_rows.shape[1]
    head_size = query_rows.shape[3]
    maxima = []
    totals = []
    weighted = []
    for head in range(heads_kv):
        cached_key_rows = rows[:, head * head_size : (head + 1) * head_size]
        cached_value_rows = rows[
            :, (heads_kv + head) * head_size : (heads_kv + head + 1) * head_size
        ].astype(jnp.float32)
        scores = (
            jnp.einsum(
                "rjd,nd->rjn",
                query_rows[:, head],
                cached_key_rows,
                preferred_element_type=jnp.float32,
            )
            * scale
        )
        keep = mask[:, None, :]
        largest = jnp.max(jnp.where(keep, scores, -1e30), axis=2)
        weights = jnp.where(keep, jnp.exp(scores - largest[:, :, None]), 0.0)
        maxima.append(largest)
        totals.append(jnp.sum(weights, axis=2))
        weighted.append(jnp.einsum("rjn,nd->rjd", weights, cached_value_rows, precision=HIGHEST))
    return (jnp.stack(maxima, 1), jnp.stack(totals, 1), jnp.stack(weighted, 1))


def finish(maxima, totals, weighted, new_score, incoming_values):
    best = jnp.maximum(jnp.max(maxima, axis=0), new_score)
    own_weight = jnp.exp(new_score - best)
    factor = jnp.exp(maxima - best[None])
    denom = own_weight + jnp.sum(factor * totals, axis=0)
    mixed = own_weight[..., None] * incoming_values + jnp.sum(factor[..., None] * weighted, axis=0)
    return mixed / denom[..., None]


def attend_migrate(query_rows, key_value_pool, block_owner, block_tokens, scale):
    replicas = lax.axis_size("replica")
    mine = lax.axis_index("replica")
    kv_width = key_value_pool.shape[2]
    target = block_owner // DEVICE_REQUESTS
    request = block_owner % DEVICE_REQUESTS
    leaving = target != mine
    to_replica = (
        (target[:, None] == jnp.arange(replicas, dtype=jnp.int32)[None, :]) & leaving[:, None]
    ).astype(jnp.int32)
    before = jnp.cumsum(to_replica, axis=0) - to_replica
    place = target * MIG + jnp.sum(before * to_replica, axis=1)
    select = (place[None, :] == jnp.arange(replicas * MIG, dtype=jnp.int32)[:, None]) & leaving[
        None, :
    ]
    chosen = select.astype(jnp.int32)
    send_blocks = jnp.dot(
        select.astype(jnp.bfloat16),
        key_value_pool.reshape(DEVICE_BLOCKS, BLOCK_SLOTS * kv_width),
        preferred_element_type=jnp.float32,
    ).astype(jnp.bfloat16)
    send_request = jnp.sum(chosen * request[None, :], axis=1)
    send_count = jnp.sum(chosen * block_tokens[None, :], axis=1)
    got_blocks, got_request, got_count = (
        lax.all_to_all(
            send_blocks.reshape(replicas, MIG, BLOCK_SLOTS * kv_width),
            "replica",
            split_axis=0,
            concat_axis=0,
            tiled=True,
        ),
        lax.all_to_all(
            send_request.reshape(replicas, MIG), "replica", split_axis=0, concat_axis=0, tiled=True
        ),
        lax.all_to_all(
            send_count.reshape(replicas, MIG), "replica", split_axis=0, concat_axis=0, tiled=True
        ),
    )
    positions = jnp.arange(BLOCK_SLOTS, dtype=jnp.int32)
    requests = jnp.arange(DEVICE_REQUESTS, dtype=jnp.int32)
    local_valid = (positions[None, :] < block_tokens[:, None]).reshape(-1)
    local_owner = jnp.repeat(block_owner, BLOCK_SLOTS)
    local_mask = (local_owner[None, :] == mine * DEVICE_REQUESTS + requests[:, None]) & local_valid[
        None, :
    ]
    local_state = partial_state(
        query_rows, key_value_pool.reshape(DEVICE_BLOCKS * BLOCK_SLOTS, kv_width), local_mask, scale
    )
    got_valid = (positions[None, :] < got_count.reshape(-1)[:, None]).reshape(-1)
    got_owner = jnp.repeat(got_request.reshape(-1), BLOCK_SLOTS)
    got_mask = (got_owner[None, :] == requests[:, None]) & got_valid[None, :]
    got_state = partial_state(query_rows, got_blocks.reshape(-1, kv_width), got_mask, scale)
    maxima = jnp.stack([local_state[0], got_state[0]], axis=0)
    totals = jnp.stack([local_state[1], got_state[1]], axis=0)
    weighted = jnp.stack([local_state[2], got_state[2]], axis=0)
    return (maxima, totals, weighted)


def expert_local(rows, w_gate_up, w_down):
    quarter = w_down.shape[0]
    halves = jnp.dot(rows, w_gate_up, preferred_element_type=jnp.float32)
    activation = (jax.nn.silu(halves[:, :quarter]) * halves[:, quarter:]).astype(jnp.bfloat16)
    return jnp.dot(activation, w_down, preferred_element_type=jnp.float32).astype(jnp.bfloat16)


def mixture(moe_input, expert_ids, route_weight, expert_slot, w_gate_up, w_down):
    token_rows = moe_input.shape[0]
    width = moe_input.shape[1]
    top_k = expert_ids.shape[1]
    experts = expert_slot.shape[0]
    replicas = lax.axis_size("replica")
    columns = lax.axis_size("expert")
    capacity = min(token_rows, max(2, 2 * token_rows * top_k // experts))
    flat_ids = expert_ids.reshape(-1)
    onehot = (flat_ids[:, None] == jnp.arange(experts, dtype=jnp.int32)[None, :]).astype(jnp.int32)
    before = jnp.cumsum(onehot, axis=0) - onehot
    position = jnp.sum(before * onehot, axis=1)
    slot_of = jnp.sum(onehot * expert_slot[None, :], axis=1)
    target = slot_of * capacity + position
    assign = (target[:, None] == jnp.arange(experts * capacity, dtype=jnp.int32)[None, :]).reshape(
        token_rows, top_k, experts * capacity
    )
    dispatch_map = jnp.sum(assign.astype(jnp.int32), axis=1).astype(jnp.bfloat16)
    send_rows = jnp.einsum(
        "tc,td->cd", dispatch_map, moe_input, preferred_element_type=jnp.float32
    ).astype(jnp.bfloat16)
    send = jnp.broadcast_to(
        send_rows.reshape(experts, 1, capacity, width), (experts, QUART, capacity, width)
    )
    send = send.reshape(replicas, columns, capacity, width)
    received = lax.all_to_all(
        lax.all_to_all(send, "replica", split_axis=0, concat_axis=0, tiled=True),
        "expert",
        split_axis=1,
        concat_axis=1,
        tiled=True,
    )
    quarter_part = expert_local(received.reshape(-1, width), w_gate_up, w_down)
    returned = lax.all_to_all(
        lax.all_to_all(
            quarter_part.reshape(send.shape), "replica", split_axis=0, concat_axis=0, tiled=True
        ),
        "expert",
        split_axis=1,
        concat_axis=1,
        tiled=True,
    )
    expert_out = jnp.sum(
        returned.reshape(experts, QUART, capacity, width).astype(jnp.float32), axis=1
    ).reshape(experts * capacity, width)
    mixing = jnp.sum(assign.astype(jnp.float32) * route_weight[:, :, None], axis=1)
    return jnp.dot(
        mixing, expert_out, precision=HIGHEST, preferred_element_type=jnp.float32
    ).astype(jnp.bfloat16)


def shards(
    moe_input,
    expert_ids,
    route_weight,
    expert_slot,
    w_gate_up,
    w_down,
    queries,
    incoming_key_value,
    key_value_pool,
    block_owner,
    block_tokens,
):
    moe_out = mixture(moe_input, expert_ids, route_weight, expert_slot, w_gate_up, w_down)
    scale = 1.0 / math.sqrt(HEAD_DIMENSION)
    query_rows = queries.reshape(
        DEVICE_REQUESTS, KEY_VALUE_HEADS, QUERY_HEADS // KEY_VALUE_HEADS, HEAD_DIMENSION
    )
    latest_keys = incoming_key_value[:, : KEY_VALUE_HEADS * HEAD_DIMENSION].reshape(
        DEVICE_REQUESTS, KEY_VALUE_HEADS, HEAD_DIMENSION
    )
    new_score = (
        jnp.einsum("rgjd,rgd->rgj", query_rows, latest_keys, preferred_element_type=jnp.float32)
        * scale
    )
    incoming_values = (
        incoming_key_value[:, KEY_VALUE_HEADS * HEAD_DIMENSION :]
        .reshape(DEVICE_REQUESTS, KEY_VALUE_HEADS, 1, HEAD_DIMENSION)
        .astype(jnp.float32)
    )
    maxima, totals, weighted = attend_migrate(
        query_rows, key_value_pool, block_owner, block_tokens, scale
    )
    attn_out = (
        finish(maxima, totals, weighted, new_score, incoming_values)
        .reshape(DEVICE_REQUESTS, QUERY_HEADS * HEAD_DIMENSION)
        .astype(jnp.bfloat16)
    )
    return (moe_out, attn_out)


def solution(mesh):
    placed = (
        P(("replica", "expert"), None),
        P(("replica", "expert"), None),
        P(("replica", "expert"), None),
        P(),
        P(None, ("replica", "expert")),
        P(("replica", "expert"), None),
        P(("replica", "expert"), None),
        P(("replica", "expert"), None),
        P(("replica", "expert"), None, None),
        P(("replica", "expert")),
        P(("replica", "expert")),
    )
    return jax.shard_map(
        shards,
        mesh=mesh,
        in_specs=placed,
        out_specs=(P(("replica", "expert"), None), P(("replica", "expert"), None)),
        check_vma=False,
    )
```

profile of v0, /device:TPU:0, one launch (start us, length us, event | category | flops | bytes accessed | tf_op | source)
XLA Modules:
  0.0 208.2 jit_solution(17856947573708979390)
XLA Ops:
  0.6 0.9 copy.114
  1.5 0.1 eq.95
  1.6 0.1 fusion.20
  1.7 0.2 reduce_window_sum.22
  1.9 0.8 select_reduce_fusion.10
  2.8 0.1 convert_reduce_fusion.1
  2.9 1.2 convolution_convert_fusion.2
  4.1 0.2 broadcast_in_dim.136
  4.3 30.3 %all_to_all.43 = bf16[4,8,16,2048]{3,2,1,0:T(8,128)(2,1)S(1)} all-to-all(bf16[4,8,16,2048]{3,2,1,0:T(8,128)(2,1)S(1)} %bitcast.192), channel_id=1, replica_groups=mesh['replica'=4,'expert'=8] {'replica'}, dimensions={0} | all-to-all | bytes 4194304 | tf_op jit(solution)/shard_map/all_to_all | solution.py:150
  34.7 1.4 copy.116
  36.1 4.9 %all-to-all-start.1 = ((bf16[4,8,16,2048]{3,2,0,1:T(8,128)(2,1)}), bf16[4,8,16,2048]{3,2,0,1:T(8,128)(2,1)}, u32[]{:S(2)}, u32[]{:S(2)}) async-start(bf16[4,8,16,2048]{3,2,0,1:T(8,128)(2,1)} %copy.116), calls=%async_computation.1 | async-start | bytes 4194304 | tf_op jit(solution)/shard_map/all_to_all | solution.py:149
  41.0 4.1 %copy.148 = bf16[2,8,64,1024]{3,1,2,0:T(8,128)(2,1)} copy(bf16[2,8,64,1024]{3,2,1,0:T(8,128)(2,1)} %bitcast.195) | data formatting | bytes 4194304
  45.2 0.2 select_reduce_fusion.11
  45.4 2.0 convolution_convert_fusion
  47.5 1.6 reshape.247
  49.1 0.1 select_reduce_fusion.13
  49.3 0.7 all_to_all.33
  50.0 40.1 %all-to-all-done.1 = bf16[4,8,16,2048]{3,2,0,1:T(8,128)(2,1)} async-done(((bf16[4,8,16,2048]{3,2,0,1:T(8,128)(2,1)}), bf16[4,8,16,2048]{3,2,0,1:T(8,128)(2,1)}, u32[]{:S(2)}, u32[]{:S(2)}) %all-to-all-start.1) | async-done | bytes 2097184 | tf_op jit(solution)/shard_map/all_to_all | solution.py:149
  90.2 3.2 %all-to-all-start.5 = ((s32[4,1,2]{2,1,0:T(1,128)}), s32[4,1,2]{2,1,0:T(1,128)S(1)}, u32[]{:S(2)}, u32[]{:S(2)}) async-start(s32[4,1,2]{2,1,0:T(1,128)} %bitcast.26), calls=%async_computation.5 | async-start | bytes 4096 | tf_op jit(solution)/shard_map/all_to_all | solution.py:93
  93.4 1.7 copy.117
  95.1 1.0 fusion.63
  96.3 2.1 %convolution_convert_fusion.1 = bf16[512,2048]{1,0:T(8,128)(2,1)} fusion(bf16[192,2048]{1,0:T(8,128)(2,1)S(1)} %copy-done.6, f32[512,384]{0,1:T(8,128)S(1)} %fusion.63), kind=kOutput, calls=%fused_computation.2 | convolution fusion | flops 404291584 | bytes 3670016 | tf_op jit(solution)/shard_map/dot_general | solution.py:121
  98.4 8.6 %all_to_all.44 = s32[4,1,2]{2,1,0:T(1,128)S(1)} all-to-all(s32[4,1,2]{2,1,0:T(1,128)S(1)} %bitcast.231), channel_id=1, replica_groups=mesh['replica'=4,'expert'=8] {'replica'}, dimensions={0} | all-to-all | bytes 64 | tf_op jit(solution)/shard_map/all_to_all | solution.py:90
  107.0 4.4 %all-to-all-start.2 = ((bf16[4,8,16,2048]{3,2,1,0:T(8,128)(2,1)}), bf16[4,8,16,2048]{3,2,1,0:T(8,128)(2,1)}, u32[]{:S(2)}, u32[]{:S(2)}) async-start(bf16[4,8,16,2048]{3,2,1,0:T(8,128)(2,1)} %bitcast.206), calls=%async_computation.2 | async-start | bytes 4194304 | tf_op jit(solution)/shard_map/all_to_all | solution.py:158
  111.5 0.1 lt.51
  111.8 1.1 convolution_multiply_fusion
  113.0 1.1 convolution_multiply_fusion.1
  114.1 1.3 select_reduce_fusion.3
  115.4 1.2 fusion.8
  116.6 0.2 fusion.9
  116.9 17.9 %all-to-all-done.2 = bf16[4,8,16,2048]{3,2,1,0:T(8,128)(2,1)} async-done(((bf16[4,8,16,2048]{3,2,1,0:T(8,128)(2,1)}), bf16[4,8,16,2048]{3,2,1,0:T(8,128)(2,1)}, u32[]{:S(2)}, u32[]{:S(2)}) %all-to-all-start.2) | async-done | bytes 2097184 | tf_op jit(solution)/shard_map/all_to_all | solution.py:158
  134.8 3.5 %all-to-all-start.6 = ((bf16[4,2,65536]{2,1,0:T(2,128)(2,1)}), bf16[4,2,65536]{2,1,0:T(2,128)(2,1)S(1)}, u32[]{:S(2)}, u32[]{:S(2)}) async-start(bf16[4,2,65536]{2,1,0:T(2,128)(2,1)} %reshape.247), calls=%async_computation.6 | async-start | bytes 2097152 | tf_op jit(solution)/shard_map/all_to_all | solution.py:83
  138.4 1.3 convolution_bitcast_fusion.4
  139.7 1.3 convolution_bitcast_fusion.5
  140.9 1.3 convolution_bitcast_fusion.6
  142.2 1.3 convolution_bitcast_fusion.7
  143.5 3.2 %copy.118 = bf16[4,8,16,2048]{3,2,0,1:T(8,128)(2,1)} copy(bf16[4,8,16,2048]{3,2,1,0:T(8,128)(2,1)} %all-to-all-done.2) | data formatting | bytes 4194304 | tf_op jit(solution)/shard_map/all_to_all | solution.py:158
  146.7 4.7 %all-to-all-done.6 = bf16[4,2,65536]{2,1,0:T(2,128)(2,1)S(1)} async-done(((bf16[4,2,65536]{2,1,0:T(2,128)(2,1)}), bf16[4,2,65536]{2,1,0:T(2,128)(2,1)S(1)}, u32[]{:S(2)}, u32[]{:S(2)}) %all-to-all-start.6) | async-done | bytes 1048608 | tf_op jit(solution)/shard_map/all_to_all | solution.py:83
  151.3 4.4 %all-to-all-start.3 = ((bf16[4,8,16,2048]{3,2,0,1:T(8,128)(2,1)}), bf16[4,8,16,2048]{3,2,0,1:T(8,128)(2,1)}, u32[]{:S(2)}, u32[]{:S(2)}) async-start(bf16[4,8,16,2048]{3,2,0,1:T(8,128)(2,1)} %copy.118), calls=%async_computation.3 | async-start | bytes 4194304 | tf_op jit(solution)/shard_map/all_to_all | solution.py:157
  155.7 0.1 select_reduce_fusion.8
  155.8 0.1 fusion.64
  156.0 0.5 broadcast.171
  156.5 0.7 reduce.8
  157.1 0.1 lt.54
  157.3 0.1 lt.57
  157.4 0.7 reduce.9
  158.1 0.1 reshape.245
  158.3 2.1 %reshape.248 = bf16[512,1024]{1,0:T(8,128)(2,1)} reshape(bf16[4,2,65536]{2,1,0:T(2,128)(2,1)S(1)} %all-to-all-done.6) | data formatting | bytes 2097152 | tf_op jit(solution)/shard_map/reshape | solution.py:110
  160.4 1.0 fusion
  161.4 1.1 fusion.1
  162.5 1.2 select_reduce_fusion.7
  163.7 1.1 fusion.25
  164.8 0.2 fusion.26
  165.1 1.1 convolution_bitcast_fusion
  166.3 1.1 convolution_bitcast_fusion.1
  167.5 1.1 convolution_bitcast_fusion.2
  168.6 1.1 convolution_bitcast_fusion.3
  169.8 0.1 fusion.7
  169.9 0.1 divide_convert_fusion
  170.0 0.6 copy.153
  170.7 34.1 %all-to-all-done.3 = bf16[4,8,16,2048]{3,2,0,1:T(8,128)(2,1)} async-done(((bf16[4,8,16,2048]{3,2,0,1:T(8,128)(2,1)}), bf16[4,8,16,2048]{3,2,0,1:T(8,128)(2,1)}, u32[]{:S(2)}, u32[]{:S(2)}) %all-to-all-start.3) | async-done | bytes 2097184 | tf_op jit(solution)/shard_map/all_to_all | solution.py:157
  204.8 1.7 copy.119
  206.5 0.4 convert_reduce_fusion
  206.9 1.2 convolution_convert_fusion.3
  (48 shorter events, 1.2 us)
Async XLA Ops:
  0.6 94.5 %copy-start = (bf16[2048,384]{1,0:T(8,128)(2,1)S(1)}, bf16[2048,384]{1,0:T(8,128)(2,1)}, u32[]{:S(2)}) copy-start(bf16[2048,384]{1,0:T(8,128)(2,1)} %param.15) | copy-start | bytes 4718596
  36.1 54.1 %all-to-all-start.1 = ((bf16[4,8,16,2048]{3,2,0,1:T(8,128)(2,1)}), bf16[4,8,16,2048]{3,2,0,1:T(8,128)(2,1)}, u32[]{:S(2)}, u32[]{:S(2)}) async-start(bf16[4,8,16,2048]{3,2,0,1:T(8,128)(2,1)} %copy.116), calls=%async_computation.1 | async-start | bytes 4194304 | tf_op jit(solution)/shard_map/all_to_all | solution.py:149
  41.0 4.1 %copy-start.2 = (s32[16]{0:T(128)S(1)}, s32[16]{0:T(128)}, u32[]{:S(2)}) copy-start(s32[16]{0:T(128)} %param.20) | copy-start | bytes 196
  45.4 3.7 %copy-start.1 = (bf16[2,8192]{1,0:T(2,128)(2,1)S(1)}, bf16[2,8192]{1,0:T(2,128)(2,1)}, u32[]{:S(2)}) copy-start(bf16[2,8192]{1,0:T(2,128)(2,1)} %param.17) | copy-start | bytes 98308
  45.4 3.7 %copy-start.5 = (s32[16]{0:T(128)S(1)}, s32[16]{0:T(128)}, u32[]{:S(2)}) copy-start(s32[16]{0:T(128)} %param.21) | copy-start | bytes 196
  90.2 8.2 %all-to-all-start.5 = ((s32[4,1,2]{2,1,0:T(1,128)}), s32[4,1,2]{2,1,0:T(1,128)S(1)}, u32[]{:S(2)}, u32[]{:S(2)}) async-start(s32[4,1,2]{2,1,0:T(1,128)} %bitcast.26), calls=%async_computation.5 | async-start | bytes 4096 | tf_op jit(solution)/shard_map/all_to_all | solution.py:93
  95.1 1.1 copy-start.6
  107.0 27.8 %all-to-all-start.2 = ((bf16[4,8,16,2048]{3,2,1,0:T(8,128)(2,1)}), bf16[4,8,16,2048]{3,2,1,0:T(8,128)(2,1)}, u32[]{:S(2)}, u32[]{:S(2)}) async-start(bf16[4,8,16,2048]{3,2,1,0:T(8,128)(2,1)} %bitcast.206), calls=%async_computation.2 | async-start | bytes 4194304 | tf_op jit(solution)/shard_map/all_to_all | solution.py:158
  113.0 25.3 %copy-start.3 = (f32[16,8]{0,1:T(8,128)S(1)}, f32[16,8]{0,1:T(8,128)}, u32[]{:S(2)}) copy-start(f32[16,8]{0,1:T(8,128)} %param.13) | copy-start | bytes 1540
  113.0 25.4 %copy-start.4 = (bf16[2,1024]{1,0:T(2,128)(2,1)S(1)}, bf16[2,1024]{1,0:T(2,128)(2,1)}, u32[]{:S(2)}) copy-start(bf16[2,1024]{1,0:T(2,128)(2,1)} %param.18) | copy-start | bytes 12292
  134.8 16.6 %all-to-all-start.6 = ((bf16[4,2,65536]{2,1,0:T(2,128)(2,1)}), bf16[4,2,65536]{2,1,0:T(2,128)(2,1)S(1)}, u32[]{:S(2)}, u32[]{:S(2)}) async-start(bf16[4,2,65536]{2,1,0:T(2,128)(2,1)} %reshape.247), calls=%async_computation.6 | async-start | bytes 2097152 | tf_op jit(solution)/shard_map/all_to_all | solution.py:83
  151.3 53.4 %all-to-all-start.3 = ((bf16[4,8,16,2048]{3,2,0,1:T(8,128)(2,1)}), bf16[4,8,16,2048]{3,2,0,1:T(8,128)(2,1)}, u32[]{:S(2)}, u32[]{:S(2)}) async-start(bf16[4,8,16,2048]{3,2,0,1:T(8,128)(2,1)} %copy.118), calls=%async_computation.3 | async-start | bytes 4194304 | tf_op jit(solution)/shard_map/all_to_all | solution.py:157
where the time goes:
time: 209 us; the launch traced here: 208 us
  waiting for transfers between devices  96.8 us (46%)
  blocking collectives  38.9 us (19%)
  matrix products  26.5 us (13%)
  starting transfers between devices  20.4 us (10%)
  local copies, waits for them, and re-layouts  20 us (10%)
  other arithmetic  4.44 us (2%)
    all_to_all x1, waiting for transfers between devices, mixture(): lax.all_to_all(lax.all_to_all(send, 'replica', split_axis=0, concat_axis=...  40.1 us
    all_to_all x1, waiting for transfers between devices, mixture(): lax.all_to_all(lax.all_to_all(quarter_part.reshape(send.shape), 'replica'...  34.1 us
    all_to_all x1, blocking collectives, mixture(): lax.all_to_all(send, 'replica', split_axis=0, concat_axis=0, tiled=True)  30.3 us
    all_to_all x1, waiting for transfers between devices, mixture(): lax.all_to_all(quarter_part.reshape(send.shape), 'replica', split_axis=0,...  17.9 us
    dot_general x8, matrix products, partial_state(): jnp.einsum('rjn,nd->rjd', weights, cached_value_rows, precision=HIGHEST)  9.63 us
    dot_general x8, matrix products, partial_state(): jnp.einsum('rjd,nd->rjn', query_rows[:, head], cached_key_rows, preferred...  9.16 us
    all_to_all x1, blocking collectives, attend_migrate(): lax.all_to_all(send_request.reshape(replicas, MIG), 'replica', split_axis...  8.59 us
    unnamed x19, local copies, waits for them, and re-layouts  5.83 us
  transfers between devices with their start and end apart: 5, of which 4 were waited for; matrix products, arithmetic and copies ran while one was open for 20% of the time, Pallas kernels for 0%

commit v1 on v0

--- a/solution.py
+++ b/solution.py
@@ -1,8 +1,11 @@
+import functools
 import math
 
 import jax
 import jax.numpy as jnp
 from jax import lax
+from jax.experimental import pallas as pl
+from jax.experimental.pallas import tpu as pltpu
 from jax.sharding import PartitionSpec as P
 
 QUART = 4
@@ -172,6 +175,425 @@
     ).astype(jnp.bfloat16)
 
 
+CORES = 2
+PAD = 128
+MESH = pl.DeviceIdType.MESH
+
+
+def fits_fused(expert_ids, expert_slot):
+    experts = expert_slot.shape[0]
+    devices = lax.axis_size("replica") * lax.axis_size("expert")
+    return (
+        expert_ids.shape[1] == experts
+        and 3 * experts <= PAD
+        and devices == experts * QUART
+        and lax.axis_size("expert") % CORES == 0
+    )
+
+
+def fused_kernel(
+    replicas,
+    depth,
+    experts,
+    slot_ref,
+    owner_ref,
+    tokens_ref,
+    x_ref,
+    ids_ref,
+    rw_ref,
+    q_ref,
+    new_ref,
+    wgu_hbm,
+    wd_hbm,
+    kv_hbm,
+    moe_ref,
+    attn_ref,
+    xb,
+    wgu,
+    wd,
+    kv,
+    pf,
+    cs,
+    cr,
+    xs,
+    xr,
+    zf,
+    zs,
+    zr,
+    qb,
+    accf,
+    accb,
+    mlb,
+    ar,
+    mr,
+    load_sem,
+    z_send,
+    z_recv,
+    r_send,
+    r_recv,
+    c_send,
+    c_recv,
+    q_send,
+    q_recv,
+    cs_send,
+    cs_recv,
+    xs_send,
+    xs_recv,
+    zs_send,
+    zs_recv,
+    a_send,
+    a_recv,
+    m_send,
+    m_recv,
+):
+    r = lax.axis_index("replica")
+    e = lax.axis_index("expert")
+    z = e // CORES
+    c = e % CORES
+    sib = 1 - c
+    rows, width = x_ref.shape
+    quarter = wd_hbm.shape[0]
+    heads = KEY_VALUE_HEADS
+    hd = HEAD_DIMENSION
+    group = QUERY_HEADS // KEY_VALUE_HEADS
+    per = DEVICE_REQUESTS * group
+    scale = 1.0 / math.sqrt(HEAD_DIMENSION)
+    sent = []
+
+    def rdev(k):
+        return ((r + k) % replicas, e)
+
+    def zdev(k):
+        return (r, ((z + k) % depth) * CORES + c)
+
+    cdev = (r, z * CORES + sib)
+
+    def remote(src, dst, ssem, rsem, dev):
+        return pltpu.make_async_remote_copy(
+            src_ref=src, dst_ref=dst, send_sem=ssem, recv_sem=rsem, device_id=dev, device_id_type=MESH
+        )
+
+    def push(*args):
+        d = remote(*args)
+        d.start()
+        sent.append(d)
+
+    loads = [
+        pltpu.make_async_copy(wgu_hbm, wgu, load_sem.at[0]),
+        pltpu.make_async_copy(wd_hbm, wd, load_sem.at[1]),
+        pltpu.make_async_copy(kv_hbm, kv, load_sem.at[2]),
+    ]
+    for d in loads:
+        d.start()
+
+    barrier = pltpu.get_barrier_semaphore()
+    for k in range(1, replicas):
+        pl.semaphore_signal(barrier, inc=1, device_id=rdev(k), device_id_type=MESH)
+    for k in range(1, depth):
+        pl.semaphore_signal(barrier, inc=1, device_id=zdev(k), device_id_type=MESH)
+    pl.semaphore_signal(barrier, inc=1, device_id=cdev, device_id_type=MESH)
+
+    lane = lax.broadcasted_iota(jnp.int32, (rows, PAD), 1)
+    mix = jnp.zeros((rows, PAD), jnp.float32)
+    for k in range(experts):
+        chosen = ids_ref[:, k : k + 1]
+        slot = jnp.zeros((rows, 1), jnp.int32)
+        for n in range(experts):
+            slot = jnp.where(chosen == n, slot_ref[n], slot)
+        mix = mix + jnp.where(lane % experts == slot, rw_ref[:, k : k + 1], 0.0)
+    high = mix.astype(jnp.bfloat16).astype(jnp.float32)
+    rest = mix - high
+    mid = rest.astype(jnp.bfloat16).astype(jnp.float32)
+    low = rest - mid
+    terms = jnp.where(lane < experts, high, jnp.where(lane < 2 * experts, mid, low))
+    xb[z, c, r, :, :width] = x_ref[...]
+    xb[z, c, r, :, width:] = terms.astype(jnp.bfloat16)
+    qb[r] = q_ref[...]
+
+    pl.semaphore_wait(barrier, replicas - 1 + depth - 1 + 1)
+
+    def xy_out(zo):
+        piece = xb.at[(z + depth - zo) % depth, c, r]
+        for k in range(1, replicas):
+            push(piece, piece, r_send.at[zo, k], r_recv.at[zo, k], rdev(k))
+
+    def core_out(zo, k):
+        piece = xb.at[(z + depth - zo) % depth, c, (r + replicas - k) % replicas]
+        push(piece, piece, c_send.at[zo, k], c_recv.at[zo, k], cdev)
+
+    own = xb.at[z, c, r]
+    for k in range(1, depth):
+        push(own, own, z_send.at[k], z_recv.at[k], zdev(k))
+    for k in range(1, replicas):
+        push(qb.at[r], qb.at[r], q_send.at[k], q_recv.at[k], rdev(k))
+    xy_out(0)
+    core_out(0, 0)
+    for zo in range(1, depth):
+        got = xb.at[(z + depth - zo) % depth, c, r]
+        remote(got, got, z_send.at[zo], z_recv.at[zo], cdev).wait_recv()
+        xy_out(zo)
+        core_out(zo, 0)
+
+    for k in range(1, replicas):
+        got = qb.at[(r + replicas - k) % replicas]
+        remote(got, got, q_send.at[k], q_recv.at[k], cdev).wait_recv()
+    loads[2].wait()
+    blocks, slots = owner_ref.shape[0], kv.shape[0] // owner_ref.shape[0]
+    keys = kv.shape[0]
+    place = lax.broadcasted_iota(jnp.int32, (1, keys), 1)
+    holder = jnp.full((1, keys), -1, jnp.int32)
+    for b in range(blocks):
+        inside = (place >= b * slots) & (place < b * slots + tokens_ref[b])
+        holder = jnp.where(inside, owner_ref[b], holder)
+    total = replicas * per
+    asker = lax.broadcasted_iota(jnp.int32, (total, 1), 0) // group
+    keep = holder == asker
+    mlane = lax.broadcasted_iota(jnp.int32, (total, PAD), 1)
+
+    def head(g, ml):
+        col = pl.ds(pl.multiple_of(g * hd, hd), hd)
+        vcol = pl.ds(pl.multiple_of((heads + g) * hd, hd), hd)
+        qg = qb[:, pl.ds(pl.multiple_of(g * per, per), per), :].reshape(total, hd)
+        scores = (
+            lax.dot_general(
+                qg, kv[:, col], (((1,), (1,)), ((), ())), preferred_element_type=jnp.float32
+            )
+            * scale
+        )
+        top = jnp.max(jnp.where(keep, scores, -1e30), axis=1, keepdims=True)
+        weights = jnp.where(keep, jnp.exp(scores - top), 0.0)
+        mass = jnp.sum(weights, axis=1, keepdims=True)
+        acc = jnp.dot(
+            weights.astype(jnp.bfloat16), kv[:, vcol], preferred_element_type=jnp.float32
+        ).reshape(replicas, per, hd)
+        accf[:, g] = acc
+        accb[:, g] = acc.astype(jnp.bfloat16)
+        return jnp.where(mlane == g, top, jnp.where(mlane == heads + g, mass, ml))
+
+    ml = lax.fori_loop(0, heads, head, jnp.zeros((total, PAD), jnp.float32))
+    mlb[...] = ml.reshape(replicas, per, PAD)
+    for k in range(1, replicas):
+        to = (r + k) % replicas
+        push(accb.at[to], ar.at[k], a_send.at[k], a_recv.at[k], rdev(k))
+        push(mlb.at[to], mr.at[k], m_send.at[k], m_recv.at[k], rdev(k))
+
+    def finish_attention():
+        for k in range(1, replicas):
+            remote(ar.at[k], ar.at[k], a_send.at[k], a_recv.at[k], cdev).wait_recv()
+            remote(mr.at[k], mr.at[k], m_send.at[k], m_recv.at[k], cdev).wait_recv()
+        plane = lax.broadcasted_iota(jnp.int32, (per, PAD), 1)
+        mls = [mlb[r]] + [mr[k] for k in range(1, replicas)]
+
+        def pick(values, n):
+            return jnp.sum(jnp.where(plane == n, values, 0.0), axis=1, keepdims=True)
+
+        def spread(n):
+            pieces = [
+                jnp.broadcast_to(
+                    new_ref[i : i + 1, n * hd : (n + 1) * hd].astype(jnp.float32), (group, hd)
+                )
+                for i in range(DEVICE_REQUESTS)
+            ]
+            return jnp.concatenate(pieces, axis=0)
+
+        for g in range(heads):
+            query = q_ref[g * per : (g + 1) * per, :].astype(jnp.float32)
+            fresh = jnp.sum(query * spread(g), axis=1, keepdims=True) * scale
+            tops = [pick(v, g) for v in mls]
+            best = fresh
+            for t in tops:
+                best = jnp.maximum(best, t)
+            weight = jnp.exp(fresh - best)
+            denom = weight
+            mixed = weight * spread(heads + g)
+            for k in range(replicas):
+                factor = jnp.exp(tops[k] - best)
+                part = accf[r, g] if k == 0 else ar[k, g].astype(jnp.float32)
+                denom = denom + factor * pick(mls[k], heads + g)
+                mixed = mixed + factor * part
+            attn_ref[g * per : (g + 1) * per, :] = (mixed / denom).astype(attn_ref.dtype)
+
+    my_slot = (r * (depth * CORES) + e) // QUART
+    chunk = CORES * replicas * rows
+    slane = lax.broadcasted_iota(jnp.int32, (chunk, PAD), 1)
+    mine = (slane % experts == my_slot) & (slane < 3 * experts)
+
+    def gather(zo):
+        for k in range(1, replicas):
+            got = xb.at[(z + depth - zo) % depth, c, (r + replicas - k) % replicas]
+            remote(got, got, r_send.at[zo, k], r_recv.at[zo, k], cdev).wait_recv()
+            core_out(zo, k)
+
+    def expert(zo):
+        zi = (z + depth - zo) % depth
+        for k in range(replicas):
+            got = xb.at[zi, sib, (r + replicas - k) % replicas]
+            remote(got, got, c_send.at[zo, k], c_recv.at[zo, k], cdev).wait_recv()
+        block = xb[zi].reshape(chunk, width + PAD)
+        gain = jnp.sum(
+            jnp.where(mine, block[:, width:].astype(jnp.float32), 0.0), axis=1, keepdims=True
+        )
+        halves = jnp.dot(block[:, :width], wgu[...], preferred_element_type=jnp.float32)
+        gate, up = halves[:, :quarter], halves[:, quarter:]
+        act = (gate / (1.0 + jnp.exp(-gate)) * up).astype(jnp.bfloat16)
+        step = width // 4
+        for n in range(4):
+            cols = slice(n * step, (n + 1) * step)
+            part = jnp.dot(act, wd[:, cols], preferred_element_type=jnp.float32) * gain
+            part = part.reshape(CORES, replicas * rows, step)
+            pf[zo, :, :, cols] = part
+            cs[zo, :, :, cols] = part.astype(jnp.bfloat16)
+        push(cs.at[zo, sib], cr.at[zo], cs_send.at[zo], cs_recv.at[zo], cdev)
+
+    def across(zo):
+        remote(cr.at[zo], cr.at[zo], cs_send.at[zo], cs_recv.at[zo], cdev).wait_recv()
+        both = pf[zo, c] + cr[zo].astype(jnp.float32)
+        pf[zo, c] = both
+        xs[zo] = both.astype(jnp.bfloat16).reshape(replicas, rows, width)
+        for k in range(1, replicas):
+            to = (r + k) % replicas
+            push(xs.at[zo, to], xr.at[zo, k], xs_send.at[zo, k], xs_recv.at[zo, k], rdev(k))
+
+    def along(zo):
+        total = pf[zo, c, pl.ds(pl.multiple_of(r * rows, rows), rows), :]
+        for k in range(1, replicas):
+            remote(
+                xr.at[zo, k], xr.at[zo, k], xs_send.at[zo, k], xs_recv.at[zo, k], cdev
+            ).wait_recv()
+            total = total + xr[zo, k].astype(jnp.float32)
+        if zo == 0:
+            zf[...] = total
+        else:
+            zs[zo] = total.astype(jnp.bfloat16)
+            push(zs.at[zo], zr.at[zo], zs_send.at[zo], zs_recv.at[zo], zdev(depth - zo))
+
+    gather(0)
+    loads[0].wait()
+    loads[1].wait()
+    for zo in range(depth):
+        expert(zo)
+        if zo >= 1:
+            across(zo - 1)
+        if zo + 1 < depth:
+            gather(zo + 1)
+        if zo >= 2:
+            along(zo - 2)
+    across(depth - 1)
+    finish_attention()
+    if depth >= 2:
+        along(depth - 2)
+    along(depth - 1)
+    result = zf[...]
+    for zo in range(1, depth):
+        remote(zr.at[zo], zr.at[zo], zs_send.at[zo], zs_recv.at[zo], cdev).wait_recv()
+        result = result + zr[zo].astype(jnp.float32)
+    moe_ref[...] = result.astype(moe_ref.dtype)
+    for d in sent:
+        d.wait_send()
+
+
+def fused(
+    moe_input,
+    expert_ids,
+    route_weight,
+    expert_slot,
+    w_gate_up,
+    w_down,
+    queries,
+    incoming_key_value,
+    key_value_pool,
+    block_owner,
+    block_tokens,
+):
+    replicas = lax.axis_size("replica")
+    depth = lax.axis_size("expert") // CORES
+    experts = expert_slot.shape[0]
+    rows, width = moe_input.shape
+    group = QUERY_HEADS // KEY_VALUE_HEADS
+    per = DEVICE_REQUESTS * group
+    hd = HEAD_DIMENSION
+    keys = key_value_pool.shape[0] * key_value_pool.shape[1]
+    q = (
+        queries.reshape(DEVICE_REQUESTS, KEY_VALUE_HEADS, group, hd)
+        .transpose(1, 0, 2, 3)
+        .reshape(KEY_VALUE_HEADS * per, hd)
+    )
+    smem = pl.BlockSpec(memory_space=pltpu.SMEM)
+    vmem = pl.BlockSpec(memory_space=pltpu.VMEM)
+    hbm = pl.BlockSpec(memory_space=pl.ANY)
+    bf, f32 = jnp.bfloat16, jnp.float32
+    dma = pltpu.SemaphoreType.DMA
+    moe_out, attn = pl.pallas_call(
+        functools.partial(fused_kernel, replicas, depth, experts),
+        out_shape=(
+            jax.ShapeDtypeStruct((rows, width), bf),
+            jax.ShapeDtypeStruct((KEY_VALUE_HEADS * per, hd), bf),
+        ),
+        in_specs=[smem] * 3 + [vmem] * 5 + [hbm] * 3,
+        out_specs=(vmem, vmem),
+        scratch_shapes=[
+            pltpu.VMEM((depth, CORES, replicas, rows, width + PAD), bf),
+            pltpu.VMEM(w_gate_up.shape, bf),
+            pltpu.VMEM(w_down.shape, bf),
+            pltpu.VMEM((keys, key_value_pool.shape[2]), bf),
+            pltpu.VMEM((depth, CORES, replicas * rows, width), f32),
+            pltpu.VMEM((depth, CORES, replicas * rows, width), bf),
+            pltpu.VMEM((depth, replicas * rows, width), bf),
+            pltpu.VMEM((depth, replicas, rows, width), bf),
+            pltpu.VMEM((depth, replicas, rows, width), bf),
+            pltpu.VMEM((rows, width), f32),
+            pltpu.VMEM((depth, rows, width), bf),
+            pltpu.VMEM((depth, rows, width), bf),
+            pltpu.VMEM((replicas, KEY_VALUE_HEADS * per, hd), bf),
+            pltpu.VMEM((replicas, KEY_VALUE_HEADS, per, hd), f32),
+            pltpu.VMEM((replicas, KEY_VALUE_HEADS, per, hd), bf),
+            pltpu.VMEM((replicas, per, PAD), f32),
+            pltpu.VMEM((replicas, KEY_VALUE_HEADS, per, hd), bf),
+            pltpu.VMEM((replicas, per, PAD), f32),
+            dma((3,)),
+            dma((depth,)),
+            dma((depth,)),
+            dma((depth, replicas)),
+            dma((depth, replicas)),
+            dma((depth, replicas)),
+            dma((depth, replicas)),
+            dma((replicas,)),
+            dma((replicas,)),
+            dma((depth,)),
+            dma((depth,)),
+            dma((depth, replicas)),
+            dma((depth, replicas)),
+            dma((depth,)),
+            dma((depth,)),
+            dma((replicas,)),
+            dma((replicas,)),
+            dma((replicas,)),
+            dma((replicas,)),
+        ],
+        compiler_params=pltpu.CompilerParams(
+            collective_id=0, has_side_effects=True, vmem_limit_bytes=48 * 1024 * 1024
+        ),
+    )(
+        expert_slot,
+        block_owner,
+        block_tokens,
+        moe_input,
+        expert_ids,
+        route_weight,
+        q,
+        incoming_key_value,
+        w_gate_up,
+        w_down,
+        key_value_pool.reshape(keys, key_value_pool.shape[2]),
+    )
+    attn_out = (
+        attn.reshape(KEY_VALUE_HEADS, DEVICE_REQUESTS, group, hd)
+        .transpose(1, 0, 2, 3)
+        .reshape(DEVICE_REQUESTS, QUERY_HEADS * hd)
+    )
+    return (moe_out, attn_out)
+
+
 def shards(
     moe_input,
     expert_ids,
@@ -185,6 +607,20 @@
     block_owner,
     block_tokens,
 ):
+    if fits_fused(expert_ids, expert_slot):
+        return fused(
+            moe_input,
+            expert_ids,
+            route_weight,
+            expert_slot,
+            w_gate_up,
+            w_down,
+            queries,
+            incoming_key_value,
+            key_value_pool,
+            block_owner,
+            block_tokens,
+        )
     moe_out = mixture(moe_input, expert_ids, route_weight, expert_slot, w_gate_up, w_down)
     scale = 1.0 / math.sqrt(HEAD_DIMENSION)
     query_rows = queries.reshape(

time: 209 us -> 53.2 us (0.25)
  waiting for transfers between devices: 96.8 us -> 0 us
  Pallas kernels: 0 us -> 40.9 us
  blocking collectives: 38.9 us -> 0 us
  matrix products: 26.5 us -> 0 us
  starting transfers between devices: 20.4 us -> 0 us
  local copies, waits for them, and re-layouts: 20 us -> 11.2 us
  other arithmetic: 4.44 us -> 0 us
    all_to_all x5 -> x0, waiting for transfers between devices: 96.8 us -> none  [the longest x1 40.1 us: mixture(): lax.all_to_all(lax.all_to_all(send, 'replica', split_axis=0, concat_axis=...]
    pallas_call x0 -> x1, Pallas kernels: none -> 40.9 us  [fused(): pl.pallas_call(functools.partial(fused_kernel, replicas, depth, experts),...]
    all_to_all x2 -> x0, blocking collectives: 38.9 us -> none  [the longest x1 30.3 us: mixture(): lax.all_to_all(send, 'replica', split_axis=0, concat_axis=0, tiled=True)]
    dot_general x22 -> x0, matrix products: 26.5 us -> none  [the longest x8 9.63 us: partial_state(): jnp.einsum('rjn,nd->rjd', weights, cached_value_rows, precision=HIGHEST)]
    all_to_all x5 -> x0, starting transfers between devices: 20.4 us -> none  [the longest x1 4.88 us: mixture(): lax.all_to_all(lax.all_to_all(send, 'replica', split_axis=0, concat_axis=...]
    all_to_all x7 -> x0, local copies, waits for them, and re-layouts: 9.35 us -> none  [the longest x1 3.19 us: mixture(): lax.all_to_all(quarter_part.reshape(send.shape), 'replica', split_axis=0,...]
    unnamed x19 -> x21, local copies, waits for them, and re-layouts: 5.83 us -> 11.2 us
    reshape x4 -> x1, local copies, waits for them, and re-layouts: 3.82 us -> 0.01 us  [fused(): queries.reshape(DEVICE_REQUESTS, KEY_VALUE_HEADS, group, hd)]
  transfers between devices with their start and end apart: 5 -> 0, of which waited for: 4 -> 0; matrix products, arithmetic and copies ran while one was open for 20% -> 0% of each run, Pallas kernels for 0% -> 0%
where the time goes in v1:
time: 53.2 us; the launch traced here: 52.8 us
  Pallas kernels  40.9 us (77%)
  local copies, waits for them, and re-layouts  11.2 us (21%)
  between operations  0.66 us (1%)
    pallas_call x1, Pallas kernels, fused(): pl.pallas_call(functools.partial(fused_kernel, replicas, depth, experts),...  40.9 us
    unnamed x21, local copies, waits for them, and re-layouts  11.2 us

profile of v1, /device:TPU:0, one launch (start us, length us, event | category | flops | bytes accessed | tf_op | source)
XLA Modules:
  0.0 52.8 jit_solution(12885799601391356392)
XLA Ops:
  0.6 0.8 %copy.14.ids_ref = s32[16,8]{1,0:T(8,128)S(1)} copy(s32[16,8]{0,1:T(8,128)} %param.12) | data formatting | bytes 1024 | tf_op args[1]
  1.4 0.8 %copy.15.rw_ref = f32[16,8]{1,0:T(8,128)S(1)} copy(f32[16,8]{0,1:T(8,128)} %param.13) | data formatting | bytes 1024 | tf_op args[2]
  2.1 0.8 %copy.17 = bf16[1,2,64,128]{3,2,1,0:T(8,128)(2,1)S(1)} copy(bf16[1,2,64,128]{3,1,2,0:T(2,128)(2,1)} %bitcast.20) | data formatting | bytes 65536
  2.9 0.0 copy-start
  2.9 1.6 %copy-done = bf16[16,64,1024]{2,1,0:T(8,128)(2,1)S(1)} copy-done((bf16[16,64,1024]{2,1,0:T(8,128)(2,1)S(1)}, bf16[16,64,1024]{2,1,0:T(8,128)(2,1)}, u32[]{:S(2)}) %copy-start) | copy-done | bytes 2097176
  4.5 0.0 copy-start.1
  4.5 1.4 %copy-done.1 = bf16[2048,384]{1,0:T(8,128)(2,1)S(1)} copy-done((bf16[2048,384]{1,0:T(8,128)(2,1)S(1)}, bf16[2048,384]{1,0:T(8,128)(2,1)}, u32[]{:S(2)}) %copy-start.1) | copy-done | bytes 1572888
  5.9 0.0 copy-start.2
  5.9 1.1 %copy-done.2 = bf16[192,2048]{1,0:T(8,128)(2,1)S(1)} copy-done((bf16[192,2048]{1,0:T(8,128)(2,1)S(1)}, bf16[192,2048]{1,0:T(8,128)(2,1)}, u32[]{:S(2)}) %copy-start.2) | copy-done | bytes 786456
  7.1 0.0 copy-start.3
  7.1 0.8 %copy-done.3 = bf16[16,2048]{1,0:T(8,128)(2,1)S(1)} copy-done((bf16[16,2048]{1,0:T(8,128)(2,1)S(1)}, bf16[16,2048]{1,0:T(8,128)(2,1)}, u32[]{:S(2)}) %copy-start.3) | copy-done | bytes 65560
  7.9 0.0 copy-start.4
  7.9 0.7 %copy-done.4 = bf16[2,1024]{1,0:T(2,128)(2,1)S(1)} copy-done((bf16[2,1024]{1,0:T(2,128)(2,1)S(1)}, bf16[2,1024]{1,0:T(2,128)(2,1)}, u32[]{:S(2)}) %copy-start.4) | copy-done | bytes 4120
  8.6 0.0 copy-start.5
  8.6 0.7 %copy-done.5 = s32[8]{0:T(128)S(1)} copy-done((s32[8]{0:T(128)S(1)}, s32[8]{0:T(128)}, u32[]{:S(2)}) %copy-start.5) | copy-done | bytes 56
  9.2 0.0 copy-start.6
  9.2 0.7 %copy-done.6 = s32[16]{0:T(128)S(1)} copy-done((s32[16]{0:T(128)S(1)}, s32[16]{0:T(128)}, u32[]{:S(2)}) %copy-start.6) | copy-done | bytes 88
  9.9 0.0 copy-start.7
  9.9 0.7 %copy-done.7 = s32[16]{0:T(128)S(1)} copy-done((s32[16]{0:T(128)S(1)}, s32[16]{0:T(128)}, u32[]{:S(2)}) %copy-start.7) | copy-done | bytes 88
  10.5 40.9 %shard_map.122 = (bf16[16,2048]{1,0:T(8,128)(2,1)S(1)}, bf16[128,128]{1,0:T(8,128)(2,1)S(1)}) custom-call(s32[8]{0:T(128)S(1)} %copy-done.5, s32[16]{0:T(128)S(1)} %copy-done.6, s32[16]{0:T(128)S(1)} %copy-done.7, bf16[16,2048]{1,0:T(8,128)(2,1)S(1)} %copy-done.3, s32[16,8]{1,0:T(8,128)S(1)} %copy.14.ids_ref, f32[16,8]{1,0:T(8,128)S(1)} %copy.15.rw_ref, ...), custom_call_target="tpu_custom_call" | custom-call | tf_op jit(solution)/shard_map/pallas_call | solution.py:526
  51.5 0.6 %copy.20 = bf16[1,2,64,128]{3,1,2,0:T(2,128)(2,1)} copy(bf16[1,2,64,128]{3,2,1,0:T(8,128)(2,1)S(1)} %bitcast.18) | data formatting | bytes 65536
  52.1 0.6 %copy.22 = bf16[16,2048]{1,0:T(8,128)(2,1)} copy(bf16[16,2048]{1,0:T(8,128)(2,1)S(1)} %get-tuple-element.8) | data formatting | bytes 131072
  (2 shorter events, 0.0 us)
Async XLA Ops:
  2.9 1.6 %copy-start = (bf16[16,64,1024]{2,1,0:T(8,128)(2,1)S(1)}, bf16[16,64,1024]{2,1,0:T(8,128)(2,1)}, u32[]{:S(2)}) copy-start(bf16[16,64,1024]{2,1,0:T(8,128)(2,1)} %param.19) | copy-start | bytes 6291460
  4.5 1.4 %copy-start.1 = (bf16[2048,384]{1,0:T(8,128)(2,1)S(1)}, bf16[2048,384]{1,0:T(8,128)(2,1)}, u32[]{:S(2)}) copy-start(bf16[2048,384]{1,0:T(8,128)(2,1)} %wgu_hbm.1) | copy-start | bytes 4718596
  5.9 1.1 %copy-start.2 = (bf16[192,2048]{1,0:T(8,128)(2,1)S(1)}, bf16[192,2048]{1,0:T(8,128)(2,1)}, u32[]{:S(2)}) copy-start(bf16[192,2048]{1,0:T(8,128)(2,1)} %wd_hbm.1) | copy-start | bytes 2359300
  7.1 0.8 %copy-start.3 = (bf16[16,2048]{1,0:T(8,128)(2,1)S(1)}, bf16[16,2048]{1,0:T(8,128)(2,1)}, u32[]{:S(2)}) copy-start(bf16[16,2048]{1,0:T(8,128)(2,1)} %x_ref.1) | copy-start | bytes 196612
  7.9 0.7 %copy-start.4 = (bf16[2,1024]{1,0:T(2,128)(2,1)S(1)}, bf16[2,1024]{1,0:T(2,128)(2,1)}, u32[]{:S(2)}) copy-start(bf16[2,1024]{1,0:T(2,128)(2,1)} %new_ref.1) | copy-start | bytes 12292
  8.6 0.7 %copy-start.5 = (s32[8]{0:T(128)S(1)}, s32[8]{0:T(128)}, u32[]{:S(2)}) copy-start(s32[8]{0:T(128)} %slot_ref.1) | copy-start | bytes 100
  9.2 0.7 %copy-start.6 = (s32[16]{0:T(128)S(1)}, s32[16]{0:T(128)}, u32[]{:S(2)}) copy-start(s32[16]{0:T(128)} %owner_ref.1) | copy-start | bytes 196
  9.9 0.7 %copy-start.7 = (s32[16]{0:T(128)S(1)}, s32[16]{0:T(128)}, u32[]{:S(2)}) copy-start(s32[16]{0:T(128)} %tokens_ref.1) | copy-start | bytes 196

commit v2 on v1

--- a/solution.py
+++ b/solution.py
@@ -177,6 +177,7 @@
 
 CORES = 2
 PAD = 128
+VMEM_LIMIT = 60 * 1024 * 1024
 MESH = pl.DeviceIdType.MESH
 
 
@@ -198,11 +199,11 @@
     slot_ref,
     owner_ref,
     tokens_ref,
-    x_ref,
     ids_ref,
     rw_ref,
     q_ref,
     new_ref,
+    x_hbm,
     wgu_hbm,
     wd_hbm,
     kv_hbm,
@@ -251,7 +252,7 @@
     z = e // CORES
     c = e % CORES
     sib = 1 - c
-    rows, width = x_ref.shape
+    rows, width = x_hbm.shape
     quarter = wd_hbm.shape[0]
     heads = KEY_VALUE_HEADS
     hd = HEAD_DIMENSION
@@ -282,6 +283,7 @@
         pltpu.make_async_copy(wgu_hbm, wgu, load_sem.at[0]),
         pltpu.make_async_copy(wd_hbm, wd, load_sem.at[1]),
         pltpu.make_async_copy(kv_hbm, kv, load_sem.at[2]),
+        pltpu.make_async_copy(x_hbm, xb.at[z, c, r, :, pl.ds(0, width)], load_sem.at[3]),
     ]
     for d in loads:
         d.start()
@@ -293,22 +295,34 @@
         pl.semaphore_signal(barrier, inc=1, device_id=zdev(k), device_id_type=MESH)
     pl.semaphore_signal(barrier, inc=1, device_id=cdev, device_id_type=MESH)
 
-    lane = lax.broadcasted_iota(jnp.int32, (rows, PAD), 1)
-    mix = jnp.zeros((rows, PAD), jnp.float32)
+    line = lax.broadcasted_iota(jnp.int32, (PAD, rows), 0)
+    mix = jnp.zeros((PAD, rows), jnp.float32)
     for k in range(experts):
-        chosen = ids_ref[:, k : k + 1]
-        slot = jnp.zeros((rows, 1), jnp.int32)
+        chosen = ids_ref[k : k + 1, :]
+        slot = jnp.zeros((1, rows), jnp.int32)
         for n in range(experts):
             slot = jnp.where(chosen == n, slot_ref[n], slot)
-        mix = mix + jnp.where(lane % experts == slot, rw_ref[:, k : k + 1], 0.0)
+        mix = mix + jnp.where(line % experts == slot, rw_ref[k : k + 1, :], 0.0)
     high = mix.astype(jnp.bfloat16).astype(jnp.float32)
     rest = mix - high
     mid = rest.astype(jnp.bfloat16).astype(jnp.float32)
     low = rest - mid
-    terms = jnp.where(lane < experts, high, jnp.where(lane < 2 * experts, mid, low))
-    xb[z, c, r, :, :width] = x_ref[...]
-    xb[z, c, r, :, width:] = terms.astype(jnp.bfloat16)
-    qb[r] = q_ref[...]
+    terms = jnp.where(line < experts, high, jnp.where(line < 2 * experts, mid, low))
+    unit = (
+        lax.broadcasted_iota(jnp.int32, (rows, rows), 0)
+        == lax.broadcasted_iota(jnp.int32, (rows, rows), 1)
+    ).astype(jnp.bfloat16)
+    xb[z, c, r, :, width:] = lax.dot_general(
+        unit,
+        terms.astype(jnp.bfloat16),
+        (((1,), (1,)), ((), ())),
+        preferred_element_type=jnp.float32,
+    ).astype(jnp.bfloat16)
+    asked = q_ref[...].astype(jnp.float32)
+    for g in range(heads):
+        pieces = [asked[:, (g * group + j) * hd : (g * group + j + 1) * hd] for j in range(group)]
+        qb[r, g * per : (g + 1) * per, :] = jnp.concatenate(pieces, axis=0).astype(jnp.bfloat16)
+    loads[3].wait()
 
     pl.semaphore_wait(barrier, replicas - 1 + depth - 1 + 1)
 
@@ -346,7 +360,8 @@
         inside = (place >= b * slots) & (place < b * slots + tokens_ref[b])
         holder = jnp.where(inside, owner_ref[b], holder)
     total = replicas * per
-    asker = lax.broadcasted_iota(jnp.int32, (total, 1), 0) // group
+    row = lax.broadcasted_iota(jnp.int32, (total, 1), 0)
+    asker = row // per * DEVICE_REQUESTS + row % DEVICE_REQUESTS
     keep = holder == asker
     mlane = lax.broadcasted_iota(jnp.int32, (total, PAD), 1)
 
@@ -387,17 +402,17 @@
         def pick(values, n):
             return jnp.sum(jnp.where(plane == n, values, 0.0), axis=1, keepdims=True)
 
+        turn = lax.broadcasted_iota(jnp.int32, (per, hd), 0) % DEVICE_REQUESTS
+
         def spread(n):
-            pieces = [
-                jnp.broadcast_to(
-                    new_ref[i : i + 1, n * hd : (n + 1) * hd].astype(jnp.float32), (group, hd)
-                )
-                for i in range(DEVICE_REQUESTS)
-            ]
-            return jnp.concatenate(pieces, axis=0)
+            values = new_ref[:, n * hd : (n + 1) * hd].astype(jnp.float32)
+            wide = values[:1]
+            for i in range(1, DEVICE_REQUESTS):
+                wide = jnp.where(turn == i, values[i : i + 1], wide)
+            return jnp.broadcast_to(wide, (per, hd))
 
         for g in range(heads):
-            query = q_ref[g * per : (g + 1) * per, :].astype(jnp.float32)
+            query = qb[r, g * per : (g + 1) * per, :].astype(jnp.float32)
             fresh = jnp.sum(query * spread(g), axis=1, keepdims=True) * scale
             tops = [pick(v, g) for v in mls]
             best = fresh
@@ -513,11 +528,6 @@
     per = DEVICE_REQUESTS * group
     hd = HEAD_DIMENSION
     keys = key_value_pool.shape[0] * key_value_pool.shape[1]
-    q = (
-        queries.reshape(DEVICE_REQUESTS, KEY_VALUE_HEADS, group, hd)
-        .transpose(1, 0, 2, 3)
-        .reshape(KEY_VALUE_HEADS * per, hd)
-    )
     smem = pl.BlockSpec(memory_space=pltpu.SMEM)
     vmem = pl.BlockSpec(memory_space=pltpu.VMEM)
     hbm = pl.BlockSpec(memory_space=pl.ANY)
@@ -529,7 +539,7 @@
             jax.ShapeDtypeStruct((rows, width), bf),
             jax.ShapeDtypeStruct((KEY_VALUE_HEADS * per, hd), bf),
         ),
-        in_specs=[smem] * 3 + [vmem] * 5 + [hbm] * 3,
+        in_specs=[smem] * 3 + [vmem] * 4 + [hbm] * 4,
         out_specs=(vmem, vmem),
         scratch_shapes=[
             pltpu.VMEM((depth, CORES, replicas, rows, width + PAD), bf),
@@ -550,7 +560,7 @@
             pltpu.VMEM((replicas, per, PAD), f32),
             pltpu.VMEM((replicas, KEY_VALUE_HEADS, per, hd), bf),
             pltpu.VMEM((replicas, per, PAD), f32),
-            dma((3,)),
+            dma((4,)),
             dma((depth,)),
             dma((depth,)),
             dma((depth, replicas)),
@@ -571,24 +581,24 @@
             dma((replicas,)),
         ],
         compiler_params=pltpu.CompilerParams(
-            collective_id=0, has_side_effects=True, vmem_limit_bytes=48 * 1024 * 1024
+            collective_id=0, has_side_effects=True, vmem_limit_bytes=VMEM_LIMIT
         ),
     )(
         expert_slot,
         block_owner,
         block_tokens,
+        expert_ids.T,
+        route_weight.T,
+        queries,
+        incoming_key_value,
         moe_input,
-        expert_ids,
-        route_weight,
-        q,
-        incoming_key_value,
         w_gate_up,
         w_down,
         key_value_pool.reshape(keys, key_value_pool.shape[2]),
     )
     attn_out = (
-        attn.reshape(KEY_VALUE_HEADS, DEVICE_REQUESTS, group, hd)
-        .transpose(1, 0, 2, 3)
+        attn.reshape(KEY_VALUE_HEADS, group, DEVICE_REQUESTS, hd)
+        .transpose(2, 0, 1, 3)
         .reshape(DEVICE_REQUESTS, QUERY_HEADS * hd)
     )
     return (moe_out, attn_out)

time: 53.2 us -> 45.6 us (0.86)
  local copies, waits for them, and re-layouts: 11.2 us -> 2.87 us
  Pallas kernels: 40.9 us -> 41.8 us
    unnamed x21 -> x2, local copies, waits for them, and re-layouts: 11.2 us -> 2.87 us
    pallas_call x1, Pallas kernels: 40.9 us -> 41.8 us  [fused(): pl.pallas_call(functools.partial(fused_kernel, replicas, depth, experts),...]
where the time goes in v2:
time: 45.6 us; the launch traced here: 45.3 us
  Pallas kernels  41.8 us (92%)
  local copies, waits for them, and re-layouts  2.87 us (6%)
  between operations  0.64 us (1%)
    pallas_call x1, Pallas kernels, fused(): pl.pallas_call(functools.partial(fused_kernel, replicas, depth, experts),...  41.8 us
    unnamed x2, local copies, waits for them, and re-layouts  2.87 us

profile of v2, /device:TPU:0, one launch (start us, length us, event | category | flops | bytes accessed | tf_op | source)
XLA Modules:
  0.0 45.3 jit_solution(10284354135311394704)
XLA Ops:
  0.6 41.8 %shard_map.122 = (bf16[16,2048]{1,0:T(8,128)(2,1)}, bf16[128,128]{1,0:T(8,128)(2,1)}) custom-call(s32[8]{0:T(128)} %slot_ref.1, s32[16]{0:T(128)} %owner_ref.1, s32[16]{0:T(128)} %tokens_ref.1, s32[8,16]{1,0:T(8,128)} %bitcast.10, f32[8,16]{1,0:T(8,128)} %bitcast.11, bf16[2,8192]{1,0:T(2,128)(2,1)} %q_ref.1, bf16[2,1024]{1,0:T(2,128)(2,1)} %new_ref.1, ...), custom_call_target="tpu_custom_call" | custom-call | tf_op jit(solution)/shard_map/pallas_call | solution.py:536
  42.4 1.5 %copy.16 = bf16[16,2048]{1,0:T(8,128)(2,1)} copy(bf16[16,2048]{1,0:T(8,128)(2,1)} %get-tuple-element.8) | data formatting | bytes 131072
  43.9 1.4 %copy.17 = bf16[2,8192]{1,0:T(2,128)(2,1)} copy(bf16[2,8192]{1,0:T(2,128)(2,1)} %bitcast.9) | data formatting | bytes 65536

commit v3 on v2

--- a/solution.py
+++ b/solution.py
@@ -177,6 +177,7 @@
 
 CORES = 2
 PAD = 128
+SIDE = 2
 VMEM_LIMIT = 60 * 1024 * 1024
 MESH = pl.DeviceIdType.MESH
 
@@ -188,6 +189,7 @@
         expert_ids.shape[1] == experts
         and 3 * experts <= PAD
         and devices == experts * QUART
+        and lax.axis_size("replica") == SIDE * SIDE
         and lax.axis_size("expert") % CORES == 0
     )
 
@@ -216,8 +218,10 @@
     pf,
     cs,
     cr,
-    xs,
-    xr,
+    xs1,
+    xr1,
+    xs2,
+    xr2,
     zf,
     zs,
     zr,
@@ -232,14 +236,18 @@
     z_recv,
     r_send,
     r_recv,
+    d_send,
+    d_recv,
     c_send,
     c_recv,
     q_send,
     q_recv,
     cs_send,
     cs_recv,
-    xs_send,
-    xs_recv,
+    xs1_send,
+    xs1_recv,
+    xs2_send,
+    xs2_recv,
     zs_send,
     zs_recv,
     a_send,
@@ -268,6 +276,11 @@
         return (r, ((z + k) % depth) * CORES + c)
 
     cdev = (r, z * CORES + sib)
+    rx = r + 1 - 2 * (r % SIDE)
+    ry = (r + SIDE) % replicas
+    rd = replicas - 1 - r
+    near = (rx, ry)
+    half = width // 2
 
     def remote(src, dst, ssem, rsem, dev):
         return pltpu.make_async_remote_copy(
@@ -326,14 +339,35 @@
 
     pl.semaphore_wait(barrier, replicas - 1 + depth - 1 + 1)
 
+    def piece(zo, core, of):
+        return xb.at[(z + depth - zo) % depth, core, of]
+
+    def part(zo, of, h):
+        cols = pl.ds(0, half) if h == 0 else pl.ds(half, width + PAD - half)
+        return xb.at[(z + depth - zo) % depth, c, of, :, cols]
+
     def xy_out(zo):
-        piece = xb.at[(z + depth - zo) % depth, c, r]
-        for k in range(1, replicas):
-            push(piece, piece, r_send.at[zo, k], r_recv.at[zo, k], rdev(k))
-
-    def core_out(zo, k):
-        piece = xb.at[(z + depth - zo) % depth, c, (r + replicas - k) % replicas]
-        push(piece, piece, c_send.at[zo, k], c_recv.at[zo, k], cdev)
+        for h in range(2):
+            p = piece(zo, c, r)
+            push(p, p, r_send.at[zo, h], r_recv.at[zo, h], (near[h], e))
+
+    def core_out(zo, n, of):
+        p = piece(zo, c, of)
+        push(p, p, c_send.at[zo, n], c_recv.at[zo, n], cdev)
+
+    def relay(zo):
+        for h in range(2):
+            p = piece(zo, c, near[h])
+            remote(p, p, r_send.at[zo, h], r_recv.at[zo, h], cdev).wait_recv()
+            p = part(zo, near[h], h)
+            push(p, p, d_send.at[zo, h], d_recv.at[zo, h], (near[1 - h], e))
+            core_out(zo, 1 + h, near[h])
+
+    def gather(zo):
+        for h in range(2):
+            p = part(zo, rd, h)
+            remote(p, p, d_send.at[zo, h], d_recv.at[zo, h], cdev).wait_recv()
+        core_out(zo, 3, rd)
 
     own = xb.at[z, c, r]
     for k in range(1, depth):
@@ -341,12 +375,16 @@
     for k in range(1, replicas):
         push(qb.at[r], qb.at[r], q_send.at[k], q_recv.at[k], rdev(k))
     xy_out(0)
-    core_out(0, 0)
-    for zo in range(1, depth):
-        got = xb.at[(z + depth - zo) % depth, c, r]
-        remote(got, got, z_send.at[zo], z_recv.at[zo], cdev).wait_recv()
+    core_out(0, 0, r)
+
+    def onward(zo):
+        p = piece(zo, c, r)
+        remote(p, p, z_send.at[zo], z_recv.at[zo], cdev).wait_recv()
         xy_out(zo)
-        core_out(zo, 0)
+        core_out(zo, 0, r)
+
+    onward(1)
+    relay(0)
 
     for k in range(1, replicas):
         got = qb.at[(r + replicas - k) % replicas]
@@ -366,9 +404,9 @@
     mlane = lax.broadcasted_iota(jnp.int32, (total, PAD), 1)
 
     def head(g, ml):
-        col = pl.ds(pl.multiple_of(g * hd, hd), hd)
-        vcol = pl.ds(pl.multiple_of((heads + g) * hd, hd), hd)
-        qg = qb[:, pl.ds(pl.multiple_of(g * per, per), per), :].reshape(total, hd)
+        col = slice(g * hd, (g + 1) * hd)
+        vcol = slice((heads + g) * hd, (heads + g + 1) * hd)
+        qg = qb[:, g * per : (g + 1) * per, :].reshape(total, hd)
         scores = (
             lax.dot_general(
                 qg, kv[:, col], (((1,), (1,)), ((), ())), preferred_element_type=jnp.float32
@@ -385,7 +423,14 @@
         accb[:, g] = acc.astype(jnp.bfloat16)
         return jnp.where(mlane == g, top, jnp.where(mlane == heads + g, mass, ml))
 
-    ml = lax.fori_loop(0, heads, head, jnp.zeros((total, PAD), jnp.float32))
+    ml = jnp.zeros((total, PAD), jnp.float32)
+    for g in range(max(heads, depth - 1)):
+        if g < heads:
+            ml = head(g, ml)
+        if g + 2 < depth:
+            onward(g + 2)
+        if g + 1 < depth:
+            relay(g + 1)
     mlb[...] = ml.reshape(replicas, per, PAD)
     for k in range(1, replicas):
         to = (r + k) % replicas
@@ -423,27 +468,26 @@
             mixed = weight * spread(heads + g)
             for k in range(replicas):
                 factor = jnp.exp(tops[k] - best)
-                part = accf[r, g] if k == 0 else ar[k, g].astype(jnp.float32)
+                share = accf[r, g] if k == 0 else ar[k, g].astype(jnp.float32)
                 denom = denom + factor * pick(mls[k], heads + g)
-                mixed = mixed + factor * part
-            attn_ref[g * per : (g + 1) * per, :] = (mixed / denom).astype(attn_ref.dtype)
+                mixed = mixed + factor * share
+            mixed = mixed / denom
+            for j in range(group):
+                cols = slice((g * group + j) * hd, (g * group + j + 1) * hd)
+                attn_ref[:, cols] = mixed[
+                    j * DEVICE_REQUESTS : (j + 1) * DEVICE_REQUESTS, :
+                ].astype(attn_ref.dtype)
 
     my_slot = (r * (depth * CORES) + e) // QUART
     chunk = CORES * replicas * rows
     slane = lax.broadcasted_iota(jnp.int32, (chunk, PAD), 1)
     mine = (slane % experts == my_slot) & (slane < 3 * experts)
 
-    def gather(zo):
-        for k in range(1, replicas):
-            got = xb.at[(z + depth - zo) % depth, c, (r + replicas - k) % replicas]
-            remote(got, got, r_send.at[zo, k], r_recv.at[zo, k], cdev).wait_recv()
-            core_out(zo, k)
-
     def expert(zo):
         zi = (z + depth - zo) % depth
-        for k in range(replicas):
-            got = xb.at[zi, sib, (r + replicas - k) % replicas]
-            remote(got, got, c_send.at[zo, k], c_recv.at[zo, k], cdev).wait_recv()
+        for n, of in enumerate((r, rx, ry, rd)):
+            p = piece(zo, sib, of)
+            remote(p, p, c_send.at[zo, n], c_recv.at[zo, n], cdev).wait_recv()
         block = xb[zi].reshape(chunk, width + PAD)
         gain = jnp.sum(
             jnp.where(mine, block[:, width:].astype(jnp.float32), 0.0), axis=1, keepdims=True
@@ -454,50 +498,66 @@
         step = width // 4
         for n in range(4):
             cols = slice(n * step, (n + 1) * step)
-            part = jnp.dot(act, wd[:, cols], preferred_element_type=jnp.float32) * gain
-            part = part.reshape(CORES, replicas * rows, step)
-            pf[zo, :, :, cols] = part
-            cs[zo, :, :, cols] = part.astype(jnp.bfloat16)
+            out = jnp.dot(act, wd[:, cols], preferred_element_type=jnp.float32) * gain
+            out = out.reshape(CORES, replicas * rows, step)
+            pf[zo, :, :, cols] = out
+            cs[zo, :, :, cols] = out.astype(jnp.bfloat16)
         push(cs.at[zo, sib], cr.at[zo], cs_send.at[zo], cs_recv.at[zo], cdev)
+
+    def mine_of(zo, of, h):
+        return pf[
+            zo, c, pl.ds(pl.multiple_of(of * rows, rows), rows), h * half : (h + 1) * half
+        ]
 
     def across(zo):
         remote(cr.at[zo], cr.at[zo], cs_send.at[zo], cs_recv.at[zo], cdev).wait_recv()
-        both = pf[zo, c] + cr[zo].astype(jnp.float32)
-        pf[zo, c] = both
-        xs[zo] = both.astype(jnp.bfloat16).reshape(replicas, rows, width)
-        for k in range(1, replicas):
-            to = (r + k) % replicas
-            push(xs.at[zo, to], xr.at[zo, k], xs_send.at[zo, k], xs_recv.at[zo, k], rdev(k))
+        pf[zo, c] = pf[zo, c] + cr[zo].astype(jnp.float32)
+        for h in range(2):
+            to = near[1 - h]
+            xs1[zo, h, 0] = mine_of(zo, rd, h).astype(jnp.bfloat16)
+            xs1[zo, h, 1] = mine_of(zo, to, h).astype(jnp.bfloat16)
+            push(xs1.at[zo, h], xr1.at[zo, h], xs1_send.at[zo, h], xs1_recv.at[zo, h], (to, e))
+
+    def around(zo):
+        for h in range(2):
+            p = xr1.at[zo, h]
+            remote(p, p, xs1_send.at[zo, h], xs1_recv.at[zo, h], cdev).wait_recv()
+            both = mine_of(zo, near[h], h) + xr1[zo, h, 0].astype(jnp.float32)
+            xs2[zo, h] = both.astype(jnp.bfloat16)
+            push(
+                xs2.at[zo, h], xr2.at[zo, h], xs2_send.at[zo, h], xs2_recv.at[zo, h], (near[h], e)
+            )
 
     def along(zo):
-        total = pf[zo, c, pl.ds(pl.multiple_of(r * rows, rows), rows), :]
-        for k in range(1, replicas):
-            remote(
-                xr.at[zo, k], xr.at[zo, k], xs_send.at[zo, k], xs_recv.at[zo, k], cdev
-            ).wait_recv()
-            total = total + xr[zo, k].astype(jnp.float32)
-        if zo == 0:
-            zf[...] = total
-        else:
-            zs[zo] = total.astype(jnp.bfloat16)
+        for h in range(2):
+            p = xr2.at[zo, h]
+            remote(p, p, xs2_send.at[zo, h], xs2_recv.at[zo, h], cdev).wait_recv()
+            cols = slice(h * half, (h + 1) * half)
+            sums = mine_of(zo, r, h) + xr1[zo, h, 1].astype(jnp.float32)
+            sums = sums + xr2[zo, h].astype(jnp.float32)
+            if zo == 0:
+                zf[:, cols] = sums
+            else:
+                zs[zo, :, cols] = sums.astype(jnp.bfloat16)
+        if zo != 0:
             push(zs.at[zo], zr.at[zo], zs_send.at[zo], zs_recv.at[zo], zdev(depth - zo))
 
     gather(0)
     loads[0].wait()
     loads[1].wait()
-    for zo in range(depth):
-        expert(zo)
-        if zo >= 1:
+    for zo in range(depth + 3):
+        if zo < depth:
+            expert(zo)
+        if 0 <= zo - 1 < depth:
             across(zo - 1)
         if zo + 1 < depth:
             gather(zo + 1)
-        if zo >= 2:
-            along(zo - 2)
-    across(depth - 1)
-    finish_attention()
-    if depth >= 2:
-        along(depth - 2)
-    along(depth - 1)
+        if 0 <= zo - 2 < depth:
+            around(zo - 2)
+        if 0 <= zo - 3 < depth:
+            along(zo - 3)
+        if zo == depth + 1:
+            finish_attention()
     result = zf[...]
     for zo in range(1, depth):
         remote(zr.at[zo], zr.at[zo], zs_send.at[zo], zs_recv.at[zo], cdev).wait_recv()
@@ -505,6 +565,15 @@
     moe_ref[...] = result.astype(moe_ref.dtype)
     for d in sent:
         d.wait_send()
+
+
+def place_results(moe_ref, attn_ref, moe_out, attn_out, sem):
+    first = pltpu.make_async_copy(moe_ref, moe_out, sem.at[0])
+    second = pltpu.make_async_copy(attn_ref, attn_out, sem.at[1])
+    first.start()
+    second.start()
+    first.wait()
+    second.wait()
 
 
 def fused(
@@ -537,7 +606,7 @@
         functools.partial(fused_kernel, replicas, depth, experts),
         out_shape=(
             jax.ShapeDtypeStruct((rows, width), bf),
-            jax.ShapeDtypeStruct((KEY_VALUE_HEADS * per, hd), bf),
+            jax.ShapeDtypeStruct(queries.shape, bf),
         ),
         in_specs=[smem] * 3 + [vmem] * 4 + [hbm] * 4,
         out_specs=(vmem, vmem),
@@ -549,8 +618,10 @@
             pltpu.VMEM((depth, CORES, replicas * rows, width), f32),
             pltpu.VMEM((depth, CORES, replicas * rows, width), bf),
             pltpu.VMEM((depth, replicas * rows, width), bf),
-            pltpu.VMEM((depth, replicas, rows, width), bf),
-            pltpu.VMEM((depth, replicas, rows, width), bf),
+            pltpu.VMEM((depth, 2, 2, rows, width // 2), bf),
+            pltpu.VMEM((depth, 2, 2, rows, width // 2), bf),
+            pltpu.VMEM((depth, 2, rows, width // 2), bf),
+            pltpu.VMEM((depth, 2, rows, width // 2), bf),
             pltpu.VMEM((rows, width), f32),
             pltpu.VMEM((depth, rows, width), bf),
             pltpu.VMEM((depth, rows, width), bf),
@@ -563,16 +634,20 @@
             dma((4,)),
             dma((depth,)),
             dma((depth,)),
-            dma((depth, replicas)),
-            dma((depth, replicas)),
+            dma((depth, 2)),
+            dma((depth, 2)),
+            dma((depth, 2)),
+            dma((depth, 2)),
             dma((depth, replicas)),
             dma((depth, replicas)),
             dma((replicas,)),
             dma((replicas,)),
             dma((depth,)),
             dma((depth,)),
-            dma((depth, replicas)),
-            dma((depth, replicas)),
+            dma((depth, 2)),
+            dma((depth, 2)),
+            dma((depth, 2)),
+            dma((depth, 2)),
             dma((depth,)),
             dma((depth,)),
             dma((replicas,)),
@@ -596,12 +671,17 @@
         w_down,
         key_value_pool.reshape(keys, key_value_pool.shape[2]),
     )
-    attn_out = (
-        attn.reshape(KEY_VALUE_HEADS, group, DEVICE_REQUESTS, hd)
-        .transpose(2, 0, 1, 3)
-        .reshape(DEVICE_REQUESTS, QUERY_HEADS * hd)
-    )
-    return (moe_out, attn_out)
+    return pl.pallas_call(
+        place_results,
+        out_shape=(
+            jax.ShapeDtypeStruct(moe_out.shape, bf),
+            jax.ShapeDtypeStruct(attn.shape, bf),
+        ),
+        in_specs=[hbm] * 2,
+        out_specs=(hbm, hbm),
+        scratch_shapes=[dma((2,))],
+        compiler_params=pltpu.CompilerParams(vmem_limit_bytes=VMEM_LIMIT),
+    )(moe_out, attn)
 
 
 def shards(

time: 45.6 us -> 48.5 us (1.064)
  Pallas kernels: 41.8 us -> 47.7 us
  local copies, waits for them, and re-layouts: 2.87 us -> 0 us
    pallas_call x0 -> x1, Pallas kernels: none -> 4.1 us  [fused(): pl.pallas_call(place_results, out_shape=(jax.ShapeDtypeStruct(moe_out.sha...]
    unnamed x2 -> x0, local copies, waits for them, and re-layouts: 2.87 us -> none
    pallas_call x1, Pallas kernels: 41.8 us -> 43.6 us  [fused(): pl.pallas_call(functools.partial(fused_kernel, replicas, depth, experts),...]
where the time goes in v3:
time: 48.5 us; the launch traced here: 48.3 us
  Pallas kernels  47.7 us (98%)
  between operations  0.64 us (1%)
    pallas_call x1, Pallas kernels, fused(): pl.pallas_call(functools.partial(fused_kernel, replicas, depth, experts),...  43.6 us
    pallas_call x1, Pallas kernels, fused(): pl.pallas_call(place_results, out_shape=(jax.ShapeDtypeStruct(moe_out.sha...  4.1 us

profile of v3, /device:TPU:0, one launch (start us, length us, event | category | flops | bytes accessed | tf_op | source)
XLA Modules:
  0.0 48.3 jit_solution(15469694014749440145)
XLA Ops:
  0.6 43.6 %shard_map.122 = (bf16[16,2048]{1,0:T(8,128)(2,1)}, bf16[2,8192]{1,0:T(2,128)(2,1)}) custom-call(s32[8]{0:T(128)} %slot_ref.1, s32[16]{0:T(128)} %owner_ref.1, s32[16]{0:T(128)} %tokens_ref.1, s32[8,16]{1,0:T(8,128)} %bitcast.4, f32[8,16]{1,0:T(8,128)} %bitcast.5, bf16[2,8192]{1,0:T(2,128)(2,1)} %q_ref.1, bf16[2,1024]{1,0:T(2,128)(2,1)} %new_ref.1, ...), custom_call_target="tpu_custom_call" | custom-call | tf_op jit(solution)/shard_map/pallas_call | solution.py:605
  44.2 4.1 %shard_map.123 = (bf16[16,2048]{1,0:T(8,128)(2,1)}, bf16[2,8192]{1,0:T(2,128)(2,1)}) custom-call(bf16[16,2048]{1,0:T(8,128)(2,1)} %get-tuple-element.4.moe_ref, bf16[2,8192]{1,0:T(2,128)(2,1)} %get-tuple-element.5.attn_ref), custom_call_target="tpu_custom_call" | custom-call | tf_op jit(solution)/shard_map/pallas_call | solution.py:674

commit v4 on v2

--- a/solution.py
+++ b/solution.py
@@ -199,16 +199,20 @@
     slot_ref,
     owner_ref,
     tokens_ref,
-    ids_ref,
-    rw_ref,
-    q_ref,
-    new_ref,
+    ids_hbm,
+    rw_hbm,
+    q_hbm,
+    new_hbm,
     x_hbm,
     wgu_hbm,
     wd_hbm,
     kv_hbm,
     moe_ref,
     attn_ref,
+    ids_ref,
+    rw_ref,
+    q_ref,
+    new_ref,
     xb,
     wgu,
     wd,
@@ -284,9 +288,13 @@
         pltpu.make_async_copy(wd_hbm, wd, load_sem.at[1]),
         pltpu.make_async_copy(kv_hbm, kv, load_sem.at[2]),
         pltpu.make_async_copy(x_hbm, xb.at[z, c, r, :, pl.ds(0, width)], load_sem.at[3]),
+        pltpu.make_async_copy(ids_hbm, ids_ref, load_sem.at[4]),
+        pltpu.make_async_copy(rw_hbm, rw_ref, load_sem.at[5]),
+        pltpu.make_async_copy(q_hbm, q_ref, load_sem.at[6]),
+        pltpu.make_async_copy(new_hbm, new_ref, load_sem.at[7]),
     ]
-    for d in loads:
-        d.start()
+    for n in (3, 4, 5, 6, 7, 2, 0, 1):
+        loads[n].start()
 
     barrier = pltpu.get_barrier_semaphore()
     for k in range(1, replicas):
@@ -295,6 +303,8 @@
         pl.semaphore_signal(barrier, inc=1, device_id=zdev(k), device_id_type=MESH)
     pl.semaphore_signal(barrier, inc=1, device_id=cdev, device_id_type=MESH)
 
+    loads[4].wait()
+    loads[5].wait()
     line = lax.broadcasted_iota(jnp.int32, (PAD, rows), 0)
     mix = jnp.zeros((PAD, rows), jnp.float32)
     for k in range(experts):
@@ -318,6 +328,7 @@
         (((1,), (1,)), ((), ())),
         preferred_element_type=jnp.float32,
     ).astype(jnp.bfloat16)
+    loads[6].wait()
     asked = q_ref[...].astype(jnp.float32)
     for g in range(heads):
         pieces = [asked[:, (g * group + j) * hd : (g * group + j + 1) * hd] for j in range(group)]
@@ -342,11 +353,15 @@
         push(qb.at[r], qb.at[r], q_send.at[k], q_recv.at[k], rdev(k))
     xy_out(0)
     core_out(0, 0)
-    for zo in range(1, depth):
+
+    def onward(zo):
         got = xb.at[(z + depth - zo) % depth, c, r]
         remote(got, got, z_send.at[zo], z_recv.at[zo], cdev).wait_recv()
         xy_out(zo)
         core_out(zo, 0)
+
+    if depth > 1:
+        onward(1)
 
     for k in range(1, replicas):
         got = qb.at[(r + replicas - k) % replicas]
@@ -366,9 +381,9 @@
     mlane = lax.broadcasted_iota(jnp.int32, (total, PAD), 1)
 
     def head(g, ml):
-        col = pl.ds(pl.multiple_of(g * hd, hd), hd)
-        vcol = pl.ds(pl.multiple_of((heads + g) * hd, hd), hd)
-        qg = qb[:, pl.ds(pl.multiple_of(g * per, per), per), :].reshape(total, hd)
+        col = slice(g * hd, (g + 1) * hd)
+        vcol = slice((heads + g) * hd, (heads + g + 1) * hd)
+        qg = qb[:, g * per : (g + 1) * per, :].reshape(total, hd)
         scores = (
             lax.dot_general(
                 qg, kv[:, col], (((1,), (1,)), ((), ())), preferred_element_type=jnp.float32
@@ -385,14 +400,15 @@
         accb[:, g] = acc.astype(jnp.bfloat16)
         return jnp.where(mlane == g, top, jnp.where(mlane == heads + g, mass, ml))
 
-    ml = lax.fori_loop(0, heads, head, jnp.zeros((total, PAD), jnp.float32))
-    mlb[...] = ml.reshape(replicas, per, PAD)
-    for k in range(1, replicas):
-        to = (r + k) % replicas
-        push(accb.at[to], ar.at[k], a_send.at[k], a_recv.at[k], rdev(k))
-        push(mlb.at[to], mr.at[k], m_send.at[k], m_recv.at[k], rdev(k))
+    def hand_back(ml):
+        mlb[...] = ml.reshape(replicas, per, PAD)
+        for k in range(1, replicas):
+            to = (r + k) % replicas
+            push(accb.at[to], ar.at[k], a_send.at[k], a_recv.at[k], rdev(k))
+            push(mlb.at[to], mr.at[k], m_send.at[k], m_recv.at[k], rdev(k))
 
     def finish_attention():
+        loads[7].wait()
         for k in range(1, replicas):
             remote(ar.at[k], ar.at[k], a_send.at[k], a_recv.at[k], cdev).wait_recv()
             remote(mr.at[k], mr.at[k], m_send.at[k], m_recv.at[k], cdev).wait_recv()
@@ -426,7 +442,12 @@
                 part = accf[r, g] if k == 0 else ar[k, g].astype(jnp.float32)
                 denom = denom + factor * pick(mls[k], heads + g)
                 mixed = mixed + factor * part
-            attn_ref[g * per : (g + 1) * per, :] = (mixed / denom).astype(attn_ref.dtype)
+            mixed = mixed / denom
+            for j in range(group):
+                cols = slice((g * group + j) * hd, (g * group + j + 1) * hd)
+                attn_ref[:, cols] = mixed[
+                    j * DEVICE_REQUESTS : (j + 1) * DEVICE_REQUESTS, :
+                ].astype(attn_ref.dtype)
 
     my_slot = (r * (depth * CORES) + e) // QUART
     chunk = CORES * replicas * rows
@@ -444,7 +465,13 @@
         for k in range(replicas):
             got = xb.at[zi, sib, (r + replicas - k) % replicas]
             remote(got, got, c_send.at[zo, k], c_recv.at[zo, k], cdev).wait_recv()
-        block = xb[zi].reshape(chunk, width + PAD)
+        block = jnp.concatenate(
+            [
+                xb[zi, sib].reshape(chunk // 2, width + PAD),
+                xb[zi, c].reshape(chunk // 2, width + PAD),
+            ],
+            axis=0,
+        )
         gain = jnp.sum(
             jnp.where(mine, block[:, width:].astype(jnp.float32), 0.0), axis=1, keepdims=True
         )
@@ -455,22 +482,21 @@
         for n in range(4):
             cols = slice(n * step, (n + 1) * step)
             part = jnp.dot(act, wd[:, cols], preferred_element_type=jnp.float32) * gain
-            part = part.reshape(CORES, replicas * rows, step)
-            pf[zo, :, :, cols] = part
-            cs[zo, :, :, cols] = part.astype(jnp.bfloat16)
-        push(cs.at[zo, sib], cr.at[zo], cs_send.at[zo], cs_recv.at[zo], cdev)
+            cs[zo, :, cols] = part[: chunk // 2].astype(jnp.bfloat16)
+            pf[zo, :, cols] = part[chunk // 2 :]
+        push(cs.at[zo], cr.at[zo], cs_send.at[zo], cs_recv.at[zo], cdev)
 
     def across(zo):
         remote(cr.at[zo], cr.at[zo], cs_send.at[zo], cs_recv.at[zo], cdev).wait_recv()
-        both = pf[zo, c] + cr[zo].astype(jnp.float32)
-        pf[zo, c] = both
+        both = pf[zo] + cr[zo].astype(jnp.float32)
+        pf[zo] = both
         xs[zo] = both.astype(jnp.bfloat16).reshape(replicas, rows, width)
         for k in range(1, replicas):
             to = (r + k) % replicas
             push(xs.at[zo, to], xr.at[zo, k], xs_send.at[zo, k], xs_recv.at[zo, k], rdev(k))
 
     def along(zo):
-        total = pf[zo, c, pl.ds(pl.multiple_of(r * rows, rows), rows), :]
+        total = pf[zo, pl.ds(pl.multiple_of(r * rows, rows), rows), :]
         for k in range(1, replicas):
             remote(
                 xr.at[zo, k], xr.at[zo, k], xs_send.at[zo, k], xs_recv.at[zo, k], cdev
@@ -482,22 +508,36 @@
             zs[zo] = total.astype(jnp.bfloat16)
             push(zs.at[zo], zr.at[zo], zs_send.at[zo], zs_recv.at[zo], zdev(depth - zo))
 
+    ml = head(0, jnp.zeros((total, PAD), jnp.float32))
+    if depth > 2:
+        onward(2)
     gather(0)
+    done = 1
+    if heads > 1:
+        ml = head(1, ml)
+        done = 2
+    for zo in range(3, depth):
+        onward(zo)
     loads[0].wait()
     loads[1].wait()
-    for zo in range(depth):
-        expert(zo)
-        if zo >= 1:
+    for zo in range(depth + 2):
+        if zo < depth:
+            expert(zo)
+        if 0 <= zo - 1 < depth:
             across(zo - 1)
         if zo + 1 < depth:
             gather(zo + 1)
-        if zo >= 2:
+        last = heads if zo == 1 else min(done + 1, heads)
+        if done < heads:
+            for g in range(done, last):
+                ml = head(g, ml)
+            done = last
+            if done == heads:
+                hand_back(ml)
+        if zo == depth + 1:
+            finish_attention()
+        if 0 <= zo - 2 < depth:
             along(zo - 2)
-    across(depth - 1)
-    finish_attention()
-    if depth >= 2:
-        along(depth - 2)
-    along(depth - 1)
     result = zf[...]
     for zo in range(1, depth):
         remote(zr.at[zo], zr.at[zo], zs_send.at[zo], zs_recv.at[zo], cdev).wait_recv()
@@ -505,6 +545,24 @@
     moe_ref[...] = result.astype(moe_ref.dtype)
     for d in sent:
         d.wait_send()
+
+
+def place_results(moe_ref, attn_ref, moe_out, attn_out, moe_v, attn_v, sem):
+    ins = [
+        pltpu.make_async_copy(moe_ref, moe_v, sem.at[0]),
+        pltpu.make_async_copy(attn_ref, attn_v, sem.at[1]),
+    ]
+    outs = [
+        pltpu.make_async_copy(moe_v, moe_out, sem.at[2]),
+        pltpu.make_async_copy(attn_v, attn_out, sem.at[3]),
+    ]
+    for d in ins:
+        d.start()
+    for i, o in zip(ins, outs):
+        i.wait()
+        o.start()
+    for o in outs:
+        o.wait()
 
 
 def fused(
@@ -537,17 +595,21 @@
         functools.partial(fused_kernel, replicas, depth, experts),
         out_shape=(
             jax.ShapeDtypeStruct((rows, width), bf),
-            jax.ShapeDtypeStruct((KEY_VALUE_HEADS * per, hd), bf),
+            jax.ShapeDtypeStruct(queries.shape, bf),
         ),
-        in_specs=[smem] * 3 + [vmem] * 4 + [hbm] * 4,
+        in_specs=[smem] * 3 + [hbm] * 8,
         out_specs=(vmem, vmem),
         scratch_shapes=[
+            pltpu.VMEM(expert_ids.shape[::-1], expert_ids.dtype),
+            pltpu.VMEM(route_weight.shape[::-1], f32),
+            pltpu.VMEM(queries.shape, bf),
+            pltpu.VMEM(incoming_key_value.shape, bf),
             pltpu.VMEM((depth, CORES, replicas, rows, width + PAD), bf),
             pltpu.VMEM(w_gate_up.shape, bf),
             pltpu.VMEM(w_down.shape, bf),
             pltpu.VMEM((keys, key_value_pool.shape[2]), bf),
-            pltpu.VMEM((depth, CORES, replicas * rows, width), f32),
-            pltpu.VMEM((depth, CORES, replicas * rows, width), bf),
+            pltpu.VMEM((depth, replicas * rows, width), f32),
+            pltpu.VMEM((depth, replicas * rows, width), bf),
             pltpu.VMEM((depth, replicas * rows, width), bf),
             pltpu.VMEM((depth, replicas, rows, width), bf),
             pltpu.VMEM((depth, replicas, rows, width), bf),
@@ -560,7 +622,7 @@
             pltpu.VMEM((replicas, per, PAD), f32),
             pltpu.VMEM((replicas, KEY_VALUE_HEADS, per, hd), bf),
             pltpu.VMEM((replicas, per, PAD), f32),
-            dma((4,)),
+            dma((8,)),
             dma((depth,)),
             dma((depth,)),
             dma((depth, replicas)),
@@ -596,12 +658,21 @@
         w_down,
         key_value_pool.reshape(keys, key_value_pool.shape[2]),
     )
-    attn_out = (
-        attn.reshape(KEY_VALUE_HEADS, group, DEVICE_REQUESTS, hd)
-        .transpose(2, 0, 1, 3)
-        .reshape(DEVICE_REQUESTS, QUERY_HEADS * hd)
-    )
-    return (moe_out, attn_out)
+    return pl.pallas_call(
+        place_results,
+        out_shape=(
+            jax.ShapeDtypeStruct(moe_out.shape, bf),
+            jax.ShapeDtypeStruct(attn.shape, bf),
+        ),
+        in_specs=[hbm] * 2,
+        out_specs=(hbm, hbm),
+        scratch_shapes=[
+            pltpu.VMEM(moe_out.shape, bf),
+            pltpu.VMEM(attn.shape, bf),
+            dma((4,)),
+        ],
+        compiler_params=pltpu.CompilerParams(vmem_limit_bytes=VMEM_LIMIT),
+    )(moe_out, attn)
 
 
 def shards(

time: 45.6 us -> 43.2 us (0.947)
  local copies, waits for them, and re-layouts: 2.87 us -> 0 us
  Pallas kernels: 41.8 us -> 42.4 us
    unnamed x2 -> x0, local copies, waits for them, and re-layouts: 2.87 us -> none
    pallas_call x0 -> x1, Pallas kernels: none -> 1.51 us  [fused(): pl.pallas_call(place_results, out_shape=(jax.ShapeDtypeStruct(moe_out.sha...]
    pallas_call x1, Pallas kernels: 41.8 us -> 40.9 us  [fused(): pl.pallas_call(functools.partial(fused_kernel, replicas, depth, experts),...]
where the time goes in v4:
time: 43.2 us; the launch traced here: 43 us
  Pallas kernels  42.4 us (98%)
  between operations  0.64 us (1%)
    pallas_call x1, Pallas kernels, fused(): pl.pallas_call(functools.partial(fused_kernel, replicas, depth, experts),...  40.9 us
    pallas_call x1, Pallas kernels, fused(): pl.pallas_call(place_results, out_shape=(jax.ShapeDtypeStruct(moe_out.sha...  1.51 us

profile of v4, /device:TPU:0, one launch (start us, length us, event | category | flops | bytes accessed | tf_op | source)
XLA Modules:
  0.0 43.0 jit_solution(13825189281843011752)
XLA Ops:
  0.6 40.9 %shard_map.122 = (bf16[16,2048]{1,0:T(8,128)(2,1)}, bf16[2,8192]{1,0:T(2,128)(2,1)}) custom-call(s32[8]{0:T(128)} %slot_ref.1, s32[16]{0:T(128)} %owner_ref.1, s32[16]{0:T(128)} %tokens_ref.1, s32[8,16]{1,0:T(8,128)} %bitcast.4, f32[8,16]{1,0:T(8,128)} %bitcast.5, bf16[2,8192]{1,0:T(2,128)(2,1)} %q_hbm.1, bf16[2,1024]{1,0:T(2,128)(2,1)} %new_hbm.1, ...), custom_call_target="tpu_custom_call" | custom-call | tf_op jit(solution)/shard_map/pallas_call | solution.py:594
  41.5 1.5 %shard_map.123 = (bf16[16,2048]{1,0:T(8,128)(2,1)}, bf16[2,8192]{1,0:T(2,128)(2,1)}) custom-call(bf16[16,2048]{1,0:T(8,128)(2,1)} %get-tuple-element.4.moe_ref, bf16[2,8192]{1,0:T(2,128)(2,1)} %get-tuple-element.5.attn_ref), custom_call_target="tpu_custom_call" | custom-call | tf_op jit(solution)/shard_map/pallas_call | solution.py:661

commit v5 on v4

--- a/solution.py
+++ b/solution.py
@@ -189,6 +189,8 @@
         and 3 * experts <= PAD
         and devices == experts * QUART
         and lax.axis_size("expert") % CORES == 0
+        and lax.axis_size("expert") >= 2 * CORES
+        and QUART % CORES == 0
     )
 
 
@@ -218,8 +220,6 @@
     wd,
     kv,
     pf,
-    cs,
-    cr,
     xs,
     xr,
     zf,
@@ -236,12 +236,10 @@
     z_recv,
     r_send,
     r_recv,
-    c_send,
-    c_recv,
+    w_send,
+    w_recv,
     q_send,
     q_recv,
-    cs_send,
-    cs_recv,
     xs_send,
     xs_recv,
     zs_send,
@@ -284,10 +282,10 @@
         sent.append(d)
 
     loads = [
-        pltpu.make_async_copy(wgu_hbm, wgu, load_sem.at[0]),
-        pltpu.make_async_copy(wd_hbm, wd, load_sem.at[1]),
+        pltpu.make_async_copy(wgu_hbm, wgu.at[:, pl.ds(0, 2 * quarter)], load_sem.at[0]),
+        pltpu.make_async_copy(wd_hbm, wd.at[pl.ds(0, quarter)], load_sem.at[1]),
         pltpu.make_async_copy(kv_hbm, kv, load_sem.at[2]),
-        pltpu.make_async_copy(x_hbm, xb.at[z, c, r, :, pl.ds(0, width)], load_sem.at[3]),
+        pltpu.make_async_copy(x_hbm, xb.at[z, r, :, pl.ds(0, width)], load_sem.at[3]),
         pltpu.make_async_copy(ids_hbm, ids_ref, load_sem.at[4]),
         pltpu.make_async_copy(rw_hbm, rw_ref, load_sem.at[5]),
         pltpu.make_async_copy(q_hbm, q_ref, load_sem.at[6]),
@@ -322,7 +320,7 @@
         lax.broadcasted_iota(jnp.int32, (rows, rows), 0)
         == lax.broadcasted_iota(jnp.int32, (rows, rows), 1)
     ).astype(jnp.bfloat16)
-    xb[z, c, r, :, width:] = lax.dot_general(
+    xb[z, r, :, width:] = lax.dot_general(
         unit,
         terms.astype(jnp.bfloat16),
         (((1,), (1,)), ((), ())),
@@ -338,27 +336,36 @@
     pl.semaphore_wait(barrier, replicas - 1 + depth - 1 + 1)
 
     def xy_out(zo):
-        piece = xb.at[(z + depth - zo) % depth, c, r]
+        piece = xb.at[(z + depth - zo) % depth, r]
         for k in range(1, replicas):
             push(piece, piece, r_send.at[zo, k], r_recv.at[zo, k], rdev(k))
 
-    def core_out(zo, k):
-        piece = xb.at[(z + depth - zo) % depth, c, (r + replicas - k) % replicas]
-        push(piece, piece, c_send.at[zo, k], c_recv.at[zo, k], cdev)
-
-    own = xb.at[z, c, r]
+    def weights_in():
+        both = [
+            (
+                wgu_hbm.at[pl.ds(n * (width // 4), width // 4)],
+                wgu.at[pl.ds(n * (width // 4), width // 4), pl.ds(2 * quarter, 2 * quarter)],
+            )
+            for n in range(4)
+        ] + [(wd_hbm, wd.at[pl.ds(quarter, quarter)])]
+        return [
+            remote(src, dst, w_send.at[n], w_recv.at[n], cdev) for n, (src, dst) in enumerate(both)
+        ]
+
+    own = xb.at[z, r]
     for k in range(1, depth):
         push(own, own, z_send.at[k], z_recv.at[k], zdev(k))
     for k in range(1, replicas):
         push(qb.at[r], qb.at[r], q_send.at[k], q_recv.at[k], rdev(k))
     xy_out(0)
-    core_out(0, 0)
+    for d in weights_in():
+        d.start()
+        sent.append(d)
 
     def onward(zo):
-        got = xb.at[(z + depth - zo) % depth, c, r]
+        got = xb.at[(z + depth - zo) % depth, r]
         remote(got, got, z_send.at[zo], z_recv.at[zo], cdev).wait_recv()
         xy_out(zo)
-        core_out(zo, 0)
 
     if depth > 1:
         onward(1)
@@ -450,50 +457,43 @@
                 ].astype(attn_ref.dtype)
 
     my_slot = (r * (depth * CORES) + e) // QUART
-    chunk = CORES * replicas * rows
-    slane = lax.broadcasted_iota(jnp.int32, (chunk, PAD), 1)
-    mine = (slane % experts == my_slot) & (slane < 3 * experts)
+    chunk = replicas * rows
 
     def gather(zo):
         for k in range(1, replicas):
-            got = xb.at[(z + depth - zo) % depth, c, (r + replicas - k) % replicas]
+            got = xb.at[(z + depth - zo) % depth, (r + replicas - k) % replicas]
             remote(got, got, r_send.at[zo, k], r_recv.at[zo, k], cdev).wait_recv()
-            core_out(zo, k)
-
-    def expert(zo):
-        zi = (z + depth - zo) % depth
-        for k in range(replicas):
-            got = xb.at[zi, sib, (r + replicas - k) % replicas]
-            remote(got, got, c_send.at[zo, k], c_recv.at[zo, k], cdev).wait_recv()
+
+    def expert(group_of):
+        tall = len(group_of) * chunk
         block = jnp.concatenate(
-            [
-                xb[zi, sib].reshape(chunk // 2, width + PAD),
-                xb[zi, c].reshape(chunk // 2, width + PAD),
-            ],
-            axis=0,
+            [xb[(z + depth - zo) % depth].reshape(chunk, width + PAD) for zo in group_of], axis=0
         )
+        slane = lax.broadcasted_iota(jnp.int32, (tall, PAD), 1)
+        mine = (slane % experts == my_slot) & (slane < 3 * experts)
         gain = jnp.sum(
             jnp.where(mine, block[:, width:].astype(jnp.float32), 0.0), axis=1, keepdims=True
         )
         halves = jnp.dot(block[:, :width], wgu[...], preferred_element_type=jnp.float32)
-        gate, up = halves[:, :quarter], halves[:, quarter:]
-        act = (gate / (1.0 + jnp.exp(-gate)) * up).astype(jnp.bfloat16)
+        acts = []
+        for n in range(CORES):
+            gate = halves[:, 2 * n * quarter : (2 * n + 1) * quarter]
+            up = halves[:, (2 * n + 1) * quarter : (2 * n + 2) * quarter]
+            acts.append((gate / (1.0 + jnp.exp(-gate)) * up).astype(jnp.bfloat16))
         step = width // 4
-        for n in range(4):
-            cols = slice(n * step, (n + 1) * step)
-            part = jnp.dot(act, wd[:, cols], preferred_element_type=jnp.float32) * gain
-            cs[zo, :, cols] = part[: chunk // 2].astype(jnp.bfloat16)
-            pf[zo, :, cols] = part[chunk // 2 :]
-        push(cs.at[zo], cr.at[zo], cs_send.at[zo], cs_recv.at[zo], cdev)
-
-    def across(zo):
-        remote(cr.at[zo], cr.at[zo], cs_send.at[zo], cs_recv.at[zo], cdev).wait_recv()
-        both = pf[zo] + cr[zo].astype(jnp.float32)
-        pf[zo] = both
-        xs[zo] = both.astype(jnp.bfloat16).reshape(replicas, rows, width)
-        for k in range(1, replicas):
-            to = (r + k) % replicas
-            push(xs.at[zo, to], xr.at[zo, k], xs_send.at[zo, k], xs_recv.at[zo, k], rdev(k))
+        for m in range(4):
+            cols = slice(m * step, (m + 1) * step)
+            part = jnp.dot(acts[0], wd[:quarter, cols], preferred_element_type=jnp.float32)
+            part = part + jnp.dot(acts[1], wd[quarter:, cols], preferred_element_type=jnp.float32)
+            part = part * gain
+            for i, zo in enumerate(group_of):
+                own_part = part[i * chunk : (i + 1) * chunk]
+                pf[zo, :, cols] = own_part
+                xs[zo, :, :, cols] = own_part.astype(jnp.bfloat16).reshape(replicas, rows, step)
+        for zo in group_of:
+            for k in range(1, replicas):
+                to = (r + k) % replicas
+                push(xs.at[zo, to], xr.at[zo, k], xs_send.at[zo, k], xs_recv.at[zo, k], rdev(k))
 
     def along(zo):
         total = pf[zo, pl.ds(pl.multiple_of(r * rows, rows), rows), :]
@@ -520,24 +520,21 @@
         onward(zo)
     loads[0].wait()
     loads[1].wait()
-    for zo in range(depth + 2):
-        if zo < depth:
-            expert(zo)
-        if 0 <= zo - 1 < depth:
-            across(zo - 1)
-        if zo + 1 < depth:
-            gather(zo + 1)
-        last = heads if zo == 1 else min(done + 1, heads)
-        if done < heads:
-            for g in range(done, last):
-                ml = head(g, ml)
-            done = last
-            if done == heads:
-                hand_back(ml)
-        if zo == depth + 1:
+    for d in weights_in():
+        d.wait_recv()
+    gather(1)
+    expert((0, 1))
+    for g in range(done, heads):
+        ml = head(g, ml)
+    hand_back(ml)
+    for zo in range(2, depth):
+        gather(zo)
+        expert((zo,))
+        along(zo - 2)
+    for zo in range(max(depth - 2, 0), depth):
+        if zo == depth - 1:
             finish_attention()
-        if 0 <= zo - 2 < depth:
-            along(zo - 2)
+        along(zo)
     result = zf[...]
     for zo in range(1, depth):
         remote(zr.at[zo], zr.at[zo], zs_send.at[zo], zs_recv.at[zo], cdev).wait_recv()
@@ -604,13 +601,11 @@
             pltpu.VMEM(route_weight.shape[::-1], f32),
             pltpu.VMEM(queries.shape, bf),
             pltpu.VMEM(incoming_key_value.shape, bf),
-            pltpu.VMEM((depth, CORES, replicas, rows, width + PAD), bf),
-            pltpu.VMEM(w_gate_up.shape, bf),
-            pltpu.VMEM(w_down.shape, bf),
+            pltpu.VMEM((depth, replicas, rows, width + PAD), bf),
+            pltpu.VMEM((width, CORES * w_gate_up.shape[1]), bf),
+            pltpu.VMEM((CORES * w_down.shape[0], width), bf),
             pltpu.VMEM((keys, key_value_pool.shape[2]), bf),
             pltpu.VMEM((depth, replicas * rows, width), f32),
-            pltpu.VMEM((depth, replicas * rows, width), bf),
-            pltpu.VMEM((depth, replicas * rows, width), bf),
             pltpu.VMEM((depth, replicas, rows, width), bf),
             pltpu.VMEM((depth, replicas, rows, width), bf),
             pltpu.VMEM((rows, width), f32),
@@ -627,12 +622,10 @@
             dma((depth,)),
             dma((depth, replicas)),
             dma((depth, replicas)),
-            dma((depth, replicas)),
-            dma((depth, replicas)),
+            dma((5,)),
+            dma((5,)),
             dma((replicas,)),
             dma((replicas,)),
-            dma((depth,)),
-            dma((depth,)),
             dma((depth, replicas)),
             dma((depth, replicas)),
             dma((depth,)),

time: 43.2 us -> 42.4 us (0.981)
  Pallas kernels: 42.4 us -> 41.6 us
    pallas_call x1, Pallas kernels: 40.9 us -> 40.1 us  [fused(): pl.pallas_call(functools.partial(fused_kernel, replicas, depth, experts),...]
where the time goes in v5:
time: 42.4 us; the launch traced here: 42.2 us
  Pallas kernels  41.6 us (98%)
  between operations  0.64 us (2%)
    pallas_call x1, Pallas kernels, fused(): pl.pallas_call(functools.partial(fused_kernel, replicas, depth, experts),...  40.1 us
    pallas_call x1, Pallas kernels, fused(): pl.pallas_call(place_results, out_shape=(jax.ShapeDtypeStruct(moe_out.sha...  1.51 us

profile of v5, /device:TPU:0, one launch (start us, length us, event | category | flops | bytes accessed | tf_op | source)
XLA Modules:
  0.0 42.2 jit_solution(626087899878129052)
XLA Ops:
  0.6 40.1 %shard_map.122 = (bf16[16,2048]{1,0:T(8,128)(2,1)}, bf16[2,8192]{1,0:T(2,128)(2,1)}) custom-call(s32[8]{0:T(128)} %slot_ref.1, s32[16]{0:T(128)} %owner_ref.1, s32[16]{0:T(128)} %tokens_ref.1, s32[8,16]{1,0:T(8,128)} %bitcast.4, f32[8,16]{1,0:T(8,128)} %bitcast.5, bf16[2,8192]{1,0:T(2,128)(2,1)} %q_hbm.1, bf16[2,1024]{1,0:T(2,128)(2,1)} %new_hbm.1, ...), custom_call_target="tpu_custom_call" | custom-call | tf_op jit(solution)/shard_map/pallas_call | solution.py:591
  40.7 1.5 %shard_map.123 = (bf16[16,2048]{1,0:T(8,128)(2,1)}, bf16[2,8192]{1,0:T(2,128)(2,1)}) custom-call(bf16[16,2048]{1,0:T(8,128)(2,1)} %get-tuple-element.4.moe_ref, bf16[2,8192]{1,0:T(2,128)(2,1)} %get-tuple-element.5.attn_ref), custom_call_target="tpu_custom_call" | custom-call | tf_op jit(solution)/shard_map/pallas_call | solution.py:654

commit v6 on v5

--- a/solution.py
+++ b/solution.py
@@ -518,15 +518,15 @@
         done = 2
     for zo in range(3, depth):
         onward(zo)
+    for g in range(done, heads):
+        ml = head(g, ml)
+    hand_back(ml)
     loads[0].wait()
     loads[1].wait()
     for d in weights_in():
         d.wait_recv()
     gather(1)
     expert((0, 1))
-    for g in range(done, heads):
-        ml = head(g, ml)
-    hand_back(ml)
     for zo in range(2, depth):
         gather(zo)
         expert((zo,))

time: 42.4 us -> 42.3 us (level)
  no operation moved by 1% of the time
where the time goes in v6:
time: 42.3 us; the launch traced here: 42.2 us
  Pallas kernels  41.5 us (98%)
  between operations  0.64 us (2%)
    pallas_call x1, Pallas kernels, fused(): pl.pallas_call(functools.partial(fused_kernel, replicas, depth, experts),...  40 us
    pallas_call x1, Pallas kernels, fused(): pl.pallas_call(place_results, out_shape=(jax.ShapeDtypeStruct(moe_out.sha...  1.51 us

profile of v6, /device:TPU:0, one launch (start us, length us, event | category | flops | bytes accessed | tf_op | source)
XLA Modules:
  0.0 42.2 jit_solution(15689253168736217005)
XLA Ops:
  0.6 40.0 %shard_map.122 = (bf16[16,2048]{1,0:T(8,128)(2,1)}, bf16[2,8192]{1,0:T(2,128)(2,1)}) custom-call(s32[8]{0:T(128)} %slot_ref.1, s32[16]{0:T(128)} %owner_ref.1, s32[16]{0:T(128)} %tokens_ref.1, s32[8,16]{1,0:T(8,128)} %bitcast.4, f32[8,16]{1,0:T(8,128)} %bitcast.5, bf16[2,8192]{1,0:T(2,128)(2,1)} %q_hbm.1, bf16[2,1024]{1,0:T(2,128)(2,1)} %new_hbm.1, ...), custom_call_target="tpu_custom_call" | custom-call | tf_op jit(solution)/shard_map/pallas_call | solution.py:591
  40.7 1.5 %shard_map.123 = (bf16[16,2048]{1,0:T(8,128)(2,1)}, bf16[2,8192]{1,0:T(2,128)(2,1)}) custom-call(bf16[16,2048]{1,0:T(8,128)(2,1)} %get-tuple-element.4.moe_ref, bf16[2,8192]{1,0:T(2,128)(2,1)} %get-tuple-element.5.attn_ref), custom_call_target="tpu_custom_call" | custom-call | tf_op jit(solution)/shard_map/pallas_call | solution.py:654

commit v7 on v6

--- a/solution.py
+++ b/solution.py
@@ -525,8 +525,9 @@
     loads[1].wait()
     for d in weights_in():
         d.wait_recv()
+    expert((0,))
     gather(1)
-    expert((0, 1))
+    expert((1,))
     for zo in range(2, depth):
         gather(zo)
         expert((zo,))

time: 42.3 us -> 42.3 us (level)
  no operation moved by 1% of the time
where the time goes in v7:
time: 42.3 us; the launch traced here: 42.2 us
  Pallas kernels  41.5 us (98%)
  between operations  0.64 us (2%)
    pallas_call x1, Pallas kernels, fused(): pl.pallas_call(functools.partial(fused_kernel, replicas, depth, experts),...  40 us
    pallas_call x1, Pallas kernels, fused(): pl.pallas_call(place_results, out_shape=(jax.ShapeDtypeStruct(moe_out.sha...  1.51 us

profile of v7, /device:TPU:0, one launch (start us, length us, event | category | flops | bytes accessed | tf_op | source)
XLA Modules:
  0.0 42.2 jit_solution(4814298187357073111)
XLA Ops:
  0.6 40.0 %shard_map.122 = (bf16[16,2048]{1,0:T(8,128)(2,1)}, bf16[2,8192]{1,0:T(2,128)(2,1)}) custom-call(s32[8]{0:T(128)} %slot_ref.1, s32[16]{0:T(128)} %owner_ref.1, s32[16]{0:T(128)} %tokens_ref.1, s32[8,16]{1,0:T(8,128)} %bitcast.4, f32[8,16]{1,0:T(8,128)} %bitcast.5, bf16[2,8192]{1,0:T(2,128)(2,1)} %q_hbm.1, bf16[2,1024]{1,0:T(2,128)(2,1)} %new_hbm.1, ...), custom_call_target="tpu_custom_call" | custom-call | tf_op jit(solution)/shard_map/pallas_call | solution.py:592
  40.7 1.5 %shard_map.123 = (bf16[16,2048]{1,0:T(8,128)(2,1)}, bf16[2,8192]{1,0:T(2,128)(2,1)}) custom-call(bf16[16,2048]{1,0:T(8,128)(2,1)} %get-tuple-element.4.moe_ref, bf16[2,8192]{1,0:T(2,128)(2,1)} %get-tuple-element.5.attn_ref), custom_call_target="tpu_custom_call" | custom-call | tf_op jit(solution)/shard_map/pallas_call | solution.py:655
